TPU v7x, 256 devices: a whole 4x4x8 slice. The times are simulated.
256 devices in a mesh: layer: 16 (over x_lo, z), latent: 16 (over x_hi, y, core).
Axes of the slice: x: 4 (x_hi: 2, x_lo: 2; x = x_hi * 2 + x_lo), y: 4, z: 8, core: 2. Of those that a mesh axis runs over, the one named last changes fastest.
Arguments:
- acts: bfloat16 [512, 16, 2304], P(None, 'layer'), may hold values from -24 to 24
- enc_weight: bfloat16 [16, 2304, 8192], P('layer', None, 'latent'), may hold values from -0.015625 to 0.015625
- dec_weight: bfloat16 [8192, 16, 2304], P('latent', 'layer'), may hold values from -0.09375 to 0.09375
- enc_bias: float32 [8192], P('latent'), may hold values from -3 to 3
- dec_bias: float32 [16, 2304], P('layer'), may hold values from -3 to 3
Outputs:
- latent_grad: float32 [512, 8192], P('layer', 'latent')
- enc_grad: bfloat16 [16, 2304, 8192], P('layer', None, 'latent')
- dec_grad: bfloat16 [8192, 16, 2304], P('latent', 'layer')
All inputs are finite; a program needn't handle non-finite values.
Results may differ from a plain program's by a relative error of at most 0.012.
Values may be sent and summed in bfloat16 or wider, within the bound.
No kernel may reach another device: no remote copies, remote signals or barrier semaphores. Data moves between devices by JAX's collectives and lax.ppermute only.
A program may use at most 64 MiB of HBM per device.

v0:
```python
import math

import jax
import jax.numpy as jnp
from jax import lax
from jax.sharding import PartitionSpec as P


def local(acts, enc_weight, dec_weight, enc_bias, dec_bias):
    tokens, layers_here, width = acts.shape
    local_latents = enc_weight.shape[2]
    flat = acts.reshape(tokens, layers_here * width)
    enc_flat = enc_weight.reshape(layers_here * width, local_latents)
    dec_flat = dec_weight.reshape(local_latents, layers_here * width)
    layer_rows = tokens // lax.axis_size("layer")
    group_rows = tokens // lax.axis_size("latent")
    partial_pre = jnp.dot(flat, enc_flat, preferred_element_type=jnp.float32)
    pre = lax.psum(partial_pre, "layer") + enc_bias[None, :]
    latents = jnp.maximum(pre, 0.0).astype(jnp.bfloat16)
    recon_share = lax.psum_scatter(
        jnp.dot(latents, dec_flat, preferred_element_type=jnp.float32),
        "latent",
        scatter_dimension=0,
        tiled=True,
    )
    first_row = lax.axis_index("latent") * group_rows
    acts_share = lax.dynamic_slice_in_dim(flat, first_row, group_rows, 0).astype(jnp.float32)
    err_share = ((recon_share + dec_bias - acts_share) / math.sqrt(tokens)).astype(jnp.bfloat16)
    piece = lax.all_gather(err_share, "latent", axis=0, tiled=True)
    back = lax.dot_general(
        piece, dec_flat, (((1,), (1,)), ((), ())), preferred_element_type=jnp.float32
    )
    grads = lax.dot_general(
        latents, piece, (((0,), (0,)), ((), ())), preferred_element_type=jnp.float32
    )
    active = latents > 0
    own_first = lax.axis_index("layer") * layer_rows
    latent_sum = lax.psum(back, "layer")
    latent_grad = lax.dynamic_slice_in_dim(latent_sum, own_first, layer_rows, 0)
    grad_pre = jnp.where(active, latent_sum, jnp.float32(0.0)).astype(jnp.bfloat16)
    enc_total = lax.dot_general(
        flat, grad_pre, (((0,), (0,)), ((), ())), preferred_element_type=jnp.float32
    )
    enc_grad = enc_total.astype(jnp.bfloat16).reshape(layers_here, width, local_latents)
    dec_grad = grads.astype(jnp.bfloat16).reshape(local_latents, layers_here, width)
    return (latent_grad, enc_grad, dec_grad)


def solution(mesh):
    in_specs = (
        P(None, "layer", None),
        P("layer", None, "latent"),
        P("latent", "layer", None),
        P("latent"),
        P("layer", None),
    )
    out_specs = (P("layer", "latent"), P("layer", None, "latent"), P("latent", "layer", None))
    return jax.shard_map(local, mesh=mesh, in_specs=in_specs, out_specs=out_specs, check_vma=False)
```

profile of v0, /device:TPU:34, one launch (start us, length us, event | category | flops | bytes accessed | tf_op | source)
XLA Modules:
  0.0 457.0 jit_solution(8715114389181909036)
XLA Ops:
  7.2 0.0 copy-start
  7.2 0.0 copy-start.2
  7.2 0.0 all-reduce.3.cloned.1.call-start
  7.2 4.9 %fusion.6 = f32[512,512]{1,0:T(8,128)} fusion(bf16[1,2304,512]{2,1,0:T(8,128)(2,1)} %param.6, bf16[512,1,2304]{2,0,1:T(8,128)(2,1)} %param.5), kind=kOutput, calls=%fused_computation.8 | convolution fusion | flops 1207959552 | bytes 5767168 | tf_op jit(solution)/shard_map/dot_general | solution.py:17
  12.1 0.0 all-reduce.3.cloned.1.call-update
  12.1 0.0 reduce-scatter.2.cloned.1.call-start
  12.2 138.4 %all-reduce.3.cloned.1.call-done = f32[512,512]{1,0:T(8,128)} async-done(((f32[512,512]{1,0:T(8,128)}), f32[512,512]{1,0:T(8,128)}) %all-reduce.3.cloned.1.call-update) | async-done | bytes 1048592 | tf_op jit(solution)/shard_map/psum | solution.py:18
  150.6 1.4 maximum_convert_fusion
  152.0 3.5 fusion.4
  155.5 0.0 reduce-scatter.2.cloned.1.call-update
  155.5 0.0 all-gather.2.cloned.1.call-start
  155.6 0.6 copy-done.1
  156.2 88.3 %reduce-scatter.2.cloned.1.call-done = f32[32,2304]{1,0:T(8,128)} async-done(((f32[512,2304]{1,0:T(8,128)}), f32[32,2304]{1,0:T(8,128)}) %reduce-scatter.2.cloned.1.call-update) | async-done | bytes 294928 | tf_op jit(solution)/shard_map/reduce_scatter | solution.py:20
  244.5 1.7 fusion.12
  246.2 0.0 all-gather.2.cloned.1.call-update
  246.2 0.0 all-reduce.5.cloned.1.call-start
  246.3 53.9 %all-gather.2.cloned.1.call-done = bf16[512,2304]{1,0:T(8,128)(2,1)} async-done(((bf16[32,2304]{1,0:T(8,128)(2,1)}), bf16[512,2304]{1,0:T(8,128)(2,1)}) %all-gather.2.cloned.1.call-update) | async-done | bytes 2359312 | tf_op jit(solution)/shard_map/all_gather | solution.py:29
  300.2 4.0 fusion.2
  304.2 0.0 all-reduce.5.cloned.1.call-update
  304.3 4.5 fusion.1
  308.8 131.1 %all-reduce.5.cloned.1.call-done = f32[512,512]{1,0:T(8,128)} async-done(((f32[512,512]{1,0:T(8,128)}), f32[512,512]{1,0:T(8,128)}) %all-reduce.5.cloned.1.call-update) | async-done | bytes 1048592 | tf_op jit(solution)/shard_map/psum | solution.py:38
  439.9 4.9 %fusion = bf16[1,2304,512]{1,2,0:T(8,128)(2,1)} fusion(bf16[512,1,2304]{2,0,1:T(8,128)(2,1)} %param.5, f32[512,512]{1,0:T(8,128)} %all-reduce.5.cloned.1.call-done, bf16[512,512]{1,0:T(8,128)(2,1)S(1)} %maximum_convert_fusion), kind=kOutput, calls=%fused_computation.2 | convolution fusion | flops 1210187776 | bytes 6291456 | tf_op jit(solution)/shard_map/dot_general | solution.py:41
  444.7 4.3 copy.8
  449.0 1.5 constant_dynamic-slice_fusion
  (4 shorter events, 0.0 us)
Async XLA Ops:
  7.2 144.8 %copy-start = (bf16[512,1,2304]{2,0,1:T(8,128)(2,1)S(1)}, bf16[512,1,2304]{2,0,1:T(8,128)(2,1)}, u32[]{:S(2)}) copy-start(bf16[512,1,2304]{2,0,1:T(8,128)(2,1)} %param.7) | copy-start | bytes 7077892
  7.2 143.4 %copy-start.2 = (f32[512]{0:T(512)S(1)}, f32[512]{0:T(512)}, u32[]{:S(2)}) copy-start(f32[512]{0:T(512)} %param.8) | copy-start | bytes 6148
  7.2 143.4 %all-reduce.3.cloned.1.call-start = ((), (), s32[]{:S(2)}) async-start(), calls=%async_computation.1 | async-start | bytes 2097152 | tf_op jit(solution)/shard_map/psum | solution.py:18
  12.1 232.4 %reduce-scatter.2.cloned.1.call-start = ((), (), s32[]{:S(2)}) async-start(), calls=%async_computation.2 | async-start | bytes 5013504 | tf_op jit(solution)/shard_map/reduce_scatter | solution.py:20
  155.5 0.7 copy-start.1
  155.5 144.7 %all-gather.2.cloned.1.call-start = ((), (), s32[]{:S(2)}) async-start(), calls=%async_computation.3 | async-start | bytes 2506752 | tf_op jit(solution)/shard_map/all_gather | solution.py:29
  246.2 193.7 %all-reduce.5.cloned.1.call-start = ((), (), s32[]{:S(2)}) async-start(), calls=%async_computation.4 | async-start | bytes 2097152 | tf_op jit(solution)/shard_map/psum | solution.py:38
Sparse Core Ops, SparseCore 0:
  12.3 138.2 all-reduce.2
  155.6 88.8 reduce-scatter.1
  247.9 52.2 all-gather.1
  304.4 135.4 all-reduce.4
where the time goes:
time: 460 us; the launch traced here: 457 us
  waiting for transfers between devices  412 us (90%)
  matrix products  21.8 us (5%)
  between operations  13.8 us (3%)
  local copies, waits for them, and re-layouts  6.38 us (1%)
    psum x1, waiting for transfers between devices, local(): pre = lax.psum(partial_pre, 'layer') + enc_bias[None, :]  138 us
    psum x1, waiting for transfers between devices, local(): latent_sum = lax.psum(back, 'layer')  131 us
    reduce_scatter x1, waiting for transfers between devices, local(): lax.psum_scatter(jnp.dot(latents, dec_flat, preferred_element_type=jnp.fl...  88.3 us
    all_gather x1, waiting for transfers between devices, local(): piece = lax.all_gather(err_share, 'latent', axis=0, tiled=True)  53.9 us
  transfers between devices with their start and end apart: 4, of which 4 were waited for; matrix products, arithmetic and copies ran while one was open for 1% of the time, Pallas kernels for 0%

commit v1 on v0

v1 whole, which is shorter than its diff:
```python
import math

import jax
import jax.numpy as jnp
from jax import lax
from jax.sharding import PartitionSpec as P

F32 = jnp.float32
BF16 = jnp.bfloat16
CORE_SWAP = [(i, i ^ 1) for i in range(16)]
CHIP_GROUPS = [list(range(c, 16, 2)) for c in range(2)]


def spread(block, axis, groups=None, count=16):
    copies = jnp.broadcast_to(block[None], (count,) + block.shape)
    return lax.all_to_all(copies, axis, 0, 0, axis_index_groups=groups)


def local(acts, enc_weight, dec_weight, enc_bias, dec_bias):
    tokens, layers_here, width = acts.shape
    local_latents = enc_weight.shape[2]
    flat = acts.reshape(tokens, width)
    enc = enc_weight.reshape(width, local_latents)
    dec = dec_weight.reshape(local_latents, width)
    rows = tokens // 16
    half = tokens // 2
    core = lax.axis_index("latent") % 2
    chip = lax.axis_index("latent") // 2
    own_half = core * half
    other_half = (1 - core) * half

    partial_pre = jnp.dot(flat, enc, preferred_element_type=F32)
    parts = lax.all_to_all(partial_pre.reshape(16, rows, local_latents), "layer", 0, 0)
    own_pre = jnp.sum(parts, axis=0) + enc_bias[None, :]
    own_latents = jnp.maximum(own_pre, 0.0).astype(BF16)
    latents = spread(own_latents, "layer").reshape(tokens, local_latents)

    send = jnp.dot(
        lax.dynamic_slice_in_dim(latents, other_half, half, 0), dec, preferred_element_type=F32
    ).astype(BF16)
    received = lax.ppermute(send, "latent", CORE_SWAP)
    kept = jnp.dot(
        lax.dynamic_slice_in_dim(latents, own_half, half, 0), dec, preferred_element_type=F32
    )
    pair = (kept + received.astype(F32)).astype(BF16)
    shares = lax.all_to_all(
        pair.reshape(8, rows, width), "latent", 0, 0, axis_index_groups=CHIP_GROUPS
    )
    recon = jnp.sum(shares.astype(F32), axis=0) + dec_bias
    acts_rows = lax.dynamic_slice_in_dim(flat, own_half + chip * rows, rows, 0).astype(F32)
    err_rows = ((recon - acts_rows) / math.sqrt(tokens)).astype(BF16)
    err_own = spread(err_rows, "latent", CHIP_GROUPS, 8).reshape(half, width)
    err_other = lax.ppermute(err_own, "latent", CORE_SWAP)
    err = jnp.where(
        core == 0,
        jnp.concatenate([err_own, err_other], 0),
        jnp.concatenate([err_other, err_own], 0),
    )

    back = lax.dot_general(err, dec, (((1,), (1,)), ((), ())), preferred_element_type=F32)
    back_parts = lax.all_to_all(
        back.astype(BF16).reshape(16, rows, local_latents), "layer", 0, 0
    )
    latent_grad = jnp.sum(back_parts.astype(F32), axis=0)
    own_grad_pre = jnp.where(own_pre > 0, latent_grad, 0.0).astype(BF16)
    grad_pre = spread(own_grad_pre, "layer").reshape(tokens, local_latents)

    dec_grad = lax.dot_general(
        latents, err, (((0,), (0,)), ((), ())), preferred_element_type=F32
    ).astype(BF16)
    enc_grad = lax.dot_general(
        flat, grad_pre, (((0,), (0,)), ((), ())), preferred_element_type=F32
    ).astype(BF16)
    return (
        latent_grad,
        enc_grad.reshape(layers_here, width, local_latents),
        dec_grad.reshape(local_latents, layers_here, width),
    )


def solution(mesh):
    in_specs = (
        P(None, "layer", None),
        P("layer", None, "latent"),
        P("latent", "layer", None),
        P("latent"),
        P("layer", None),
    )
    out_specs = (P("layer", "latent"), P("layer", None, "latent"), P("latent", "layer", None))
    return jax.shard_map(local, mesh=mesh, in_specs=in_specs, out_specs=out_specs, check_vma=False)
```

time: 460 us -> 174 us (0.38)
  waiting for transfers between devices: 412 us -> 47.3 us
  blocking collectives: 0 us -> 79.3 us
  starting transfers between devices: 0.16 us -> 16.1 us
  between operations: 13.8 us -> 0.75 us
    psum x2 -> x0, waiting for transfers between devices: 270 us -> none  [the longest x1 138 us: local(): pre = lax.psum(partial_pre, 'layer') + enc_bias[None, :]]
    reduce_scatter x1 -> x0, waiting for transfers between devices: 88.3 us -> none  [local(): lax.psum_scatter(jnp.dot(latents, dec_flat, preferred_element_type=jnp.fl...]
    all_to_all x0 -> x3, blocking collectives: none -> 79.3 us  [the longest x1 35.6 us: local(): lax.all_to_all(partial_pre.reshape(16, rows, local_latents), 'layer', 0, 0)]
    all_gather x1 -> x0, waiting for transfers between devices: 53.9 us -> none  [local(): piece = lax.all_gather(err_share, 'latent', axis=0, tiled=True)]
    all_to_all x0 -> x3, waiting for transfers between devices: none -> 41.2 us  [the longest x2 24.7 us: spread(): return lax.all_to_all(copies, axis, 0, 0, axis_index_groups=groups)]
    all_to_all x0 -> x3, starting transfers between devices: none -> 16.1 us  [the longest x2 10 us: spread(): return lax.all_to_all(copies, axis, 0, 0, axis_index_groups=groups)]
    ppermute x0 -> x2, waiting for transfers between devices: none -> 6.16 us  [the longest x1 3.19 us: local(): received = lax.ppermute(send, 'latent', CORE_SWAP)]
    dot_general x4 -> x5, matrix products: 16.9 us -> 17.2 us  [the longest x1 5.37 us: local(): lax.dot_general(latents, err, (((0,), (0,)), ((), ())), preferred_element...]
  transfers between devices with their start and end apart: 4 -> 5, of which waited for: 4 -> 5; matrix products, arithmetic and copies ran while one was open for 1% -> 4% of each run, Pallas kernels for 0% -> 0%
where the time goes in v1:
time: 174 us; the launch traced here: 173 us
  blocking collectives  79.3 us (46%)
  waiting for transfers between devices  47.3 us (27%)
  matrix products  21.7 us (12%)
  starting transfers between devices  16.1 us (9%)
  local copies, waits for them, and re-layouts  6.1 us (4%)
  other arithmetic  2.01 us (1%)
    all_to_all x1, blocking collectives, local(): lax.all_to_all(partial_pre.reshape(16, rows, local_latents), 'layer', 0, 0)  35.6 us
    all_to_all x2, waiting for transfers between devices, spread(): return lax.all_to_all(copies, axis, 0, 0, axis_index_groups=groups)  24.7 us
    all_to_all x1, blocking collectives, spread(): return lax.all_to_all(copies, axis, 0, 0, axis_index_groups=groups)  23.2 us
    all_to_all x1, blocking collectives, local(): lax.all_to_all(back.astype(BF16).reshape(16, rows, local_latents), 'layer...  20.4 us
    all_to_all x1, waiting for transfers between devices, local(): lax.all_to_all(pair.reshape(8, rows, width), 'latent', 0, 0, axis_index_g...  16.4 us
    all_to_all x2, starting transfers between devices, spread(): return lax.all_to_all(copies, axis, 0, 0, axis_index_groups=groups)  10 us
    all_to_all x1, starting transfers between devices, local(): lax.all_to_all(pair.reshape(8, rows, width), 'latent', 0, 0, axis_index_g...  6.03 us
    dot_general x1, matrix products, local(): lax.dot_general(latents, err, (((0,), (0,)), ((), ())), preferred_element...  5.37 us
  transfers between devices with their start and end apart: 5, of which 5 were waited for; matrix products, arithmetic and copies ran while one was open for 4% of the time, Pallas kernels for 0%

profile of v1, /device:TPU:34, one launch (start us, length us, event | category | flops | bytes accessed | tf_op | source)
XLA Modules:
  0.0 173.3 jit_solution(9675531869265024207)
XLA Ops:
  0.6 3.9 %fusion.8 = f32[16,32,512]{2,1,0:T(8,128)S(1)} fusion(bf16[16,32,2304]{2,1,0:T(8,128)(2,1)} %bitcast.44, bf16[1,2304,512]{2,1,0:T(8,128)(2,1)} %param.6), kind=kOutput, calls=%fused_computation.12 | convolution fusion | flops 1207959552 | bytes 5767168 | tf_op jit(solution)/shard_map/dot_general | solution.py:32
  4.6 35.6 %all_to_all.30 = f32[16,32,512]{2,1,0:T(8,128)S(1)} all-to-all(f32[16,32,512]{2,1,0:T(8,128)S(1)} %fusion.8), channel_id=1, replica_groups=mesh['layer'=16,'latent'=16] {'layer'}, dimensions={0} | all-to-all | bytes 2097152 | tf_op jit(solution)/shard_map/all_to_all | solution.py:33
  40.3 0.8 broadcast_in_dim.7
  41.2 5.1 %all-to-all-start.1 = ((bf16[16,32,512]{2,1,0:T(8,128)(2,1)}), bf16[16,32,512]{2,1,0:T(8,128)(2,1)S(1)}, u32[]{:S(2)}, u32[]{:S(2)}) async-start(bf16[16,32,512]{2,1,0:T(8,128)(2,1)} %broadcast_in_dim.7), calls=%async_computation.1 | async-start | bytes 1048576 | tf_op jit(solution)/shard_map/all_to_all | solution.py:16
  46.3 14.8 %all-to-all-done.1 = bf16[16,32,512]{2,1,0:T(8,128)(2,1)S(1)} async-done(((bf16[16,32,512]{2,1,0:T(8,128)(2,1)}), bf16[16,32,512]{2,1,0:T(8,128)(2,1)S(1)}, u32[]{:S(2)}, u32[]{:S(2)}) %all-to-all-start.1) | async-done | bytes 524320 | tf_op jit(solution)/shard_map/all_to_all | solution.py:16
  61.1 1.8 %convolution_convert_fusion.2 = bf16[256,2304]{1,0:T(8,128)(2,1)} fusion(bf16[512,1,2304]{2,0,1:T(8,128)(2,1)S(1)} %copy-done, bf16[512,512]{1,0:T(8,128)(2,1)S(1)} %bitcast.36, s32[]{:T(128)S(6)} %select_n.39), kind=kOutput, calls=%fused_computation.4 | convolution fusion | flops 604569600 | bytes 3801092 | tf_op jit(solution)/shard_map/dot_general | solution.py:38
  62.9 3.2 %collective-permute-done = bf16[256,2304]{1,0:T(8,128)(2,1)} collective-permute-done((bf16[256,2304]{1,0:T(8,128)(2,1)}, bf16[256,2304]{1,0:T(8,128)(2,1)}, u32[]{:S(2)}, u32[]{:S(2)}) %collective-permute-start) | collective-permute-done | bytes 1179680 | tf_op jit(solution)/shard_map/ppermute | solution.py:41
  66.1 3.1 %add_convert_fusion = bf16[256,2304]{1,0:T(8,128)(2,1)} fusion(bf16[256,2304]{1,0:T(8,128)(2,1)} %collective-permute-done, bf16[512,1,2304]{2,0,1:T(8,128)(2,1)S(1)} %copy-done, bf16[512,512]{1,0:T(8,128)(2,1)S(1)} %bitcast.37, s32[]{:T(128)S(6)} %select_n.38), kind=kOutput, calls=%fused_computation.15 | convolution fusion | flops 605749248 | bytes 4980740 | tf_op jit(solution)/shard_map/dot_general | solution.py:42
  69.2 6.0 %all-to-all-start.2 = ((bf16[8,32,2304]{2,1,0:T(8,128)(2,1)}), bf16[8,32,2304]{2,1,0:T(8,128)(2,1)S(1)}, u32[]{:S(2)}, u32[]{:S(2)}) async-start(bf16[8,32,2304]{2,1,0:T(8,128)(2,1)} %bitcast.5), calls=%async_computation.2 | async-start | bytes 2359296 | tf_op jit(solution)/shard_map/all_to_all | solution.py:46
  75.2 0.7 reduce
  76.0 16.4 %all-to-all-done.2 = bf16[8,32,2304]{2,1,0:T(8,128)(2,1)S(1)} async-done(((bf16[8,32,2304]{2,1,0:T(8,128)(2,1)}), bf16[8,32,2304]{2,1,0:T(8,128)(2,1)S(1)}, u32[]{:S(2)}, u32[]{:S(2)}) %all-to-all-start.2) | async-done | bytes 1179680 | tf_op jit(solution)/shard_map/all_to_all | solution.py:46
  92.4 0.1 convert_reduce_fusion
  92.5 1.0 fusion.14
  93.5 0.1 broadcast_in_dim.8
  93.6 23.2 %all_to_all.31 = bf16[8,32,2304]{2,1,0:T(8,128)(2,1)S(1)} all-to-all(bf16[8,32,2304]{2,1,0:T(8,128)(2,1)S(1)} %broadcast_in_dim.8), channel_id=1, replica_groups={{0,2,4,6,8,10,12,14},{1,3,5,7,9,11,13,15},{16,18,20,22,24,26,28,30},{17..., dimensions={0} | all-to-all | bytes 2359296 | tf_op jit(solution)/shard_map/all_to_all | solution.py:16
  116.8 3.0 %collective-permute-done.1 = bf16[256,2304]{1,0:T(8,128)(2,1)} collective-permute-done((bf16[256,2304]{1,0:T(8,128)(2,1)S(1)}, bf16[256,2304]{1,0:T(8,128)(2,1)}, u32[]{:S(2)}, u32[]{:S(2)}) %collective-permute-start.1) | collective-permute-done | bytes 1179680 | tf_op jit(solution)/shard_map/ppermute | solution.py:53
  119.8 3.1 %fusion.10 = bf16[512,512]{1,0:T(8,128)(2,1)S(1)} fusion(bf16[512,1,2304]{2,0,1:T(8,128)(2,1)S(1)} %copy-done, bf16[256,2304]{1,0:T(8,128)(2,1)} %collective-permute-done.1, bf16[256,2304]{1,0:T(8,128)(2,1)S(1)} %bitcast.40, pred[]{:T(512)S(6)} %eq.5), kind=kOutput, calls=%fused_computation.16 | convolution fusion | flops 1218838528 | bytes 5242881 | tf_op jit(solution)/shard_map/dot_general | solution.py:60
  122.9 20.4 %all_to_all.32 = bf16[16,32,512]{2,1,0:T(8,128)(2,1)S(1)} all-to-all(bf16[16,32,512]{2,1,0:T(8,128)(2,1)S(1)} %bitcast.43), channel_id=1, replica_groups=mesh['layer'=16,'latent'=16] {'layer'}, dimensions={0} | all-to-all | bytes 1048576 | tf_op jit(solution)/shard_map/all_to_all | solution.py:61
  143.5 0.9 broadcast_in_dim.9
  144.3 4.9 %all-to-all-start.5 = ((bf16[16,32,512]{2,1,0:T(8,128)(2,1)}), bf16[16,32,512]{2,1,0:T(8,128)(2,1)S(1)}, u32[]{:S(2)}, u32[]{:S(2)}) async-start(bf16[16,32,512]{2,1,0:T(8,128)(2,1)} %broadcast_in_dim.9), calls=%async_computation.5 | async-start | bytes 1048576 | tf_op jit(solution)/shard_map/all_to_all | solution.py:16
  149.2 5.4 %fusion.1 = bf16[512,1,2304]{2,0,1:T(8,128)(2,1)} fusion(bf16[512,512]{1,0:T(8,128)(2,1)S(1)} %bitcast.38, bf16[256,2304]{1,0:T(8,128)(2,1)} %collective-permute-done.1, bf16[256,2304]{1,0:T(8,128)(2,1)} %bitcast.41, pred[]{:T(512)S(6)} %eq.5), kind=kOutput, calls=%fused_computation.3 | convolution fusion | flops 1219756032 | bytes 5242881 | tf_op jit(solution)/shard_map/dot_general | solution.py:68
  154.6 9.9 %all-to-all-done.5 = bf16[16,32,512]{2,1,0:T(8,128)(2,1)S(1)} async-done(((bf16[16,32,512]{2,1,0:T(8,128)(2,1)}), bf16[16,32,512]{2,1,0:T(8,128)(2,1)S(1)}, u32[]{:S(2)}, u32[]{:S(2)}) %all-to-all-start.5) | async-done | bytes 524320 | tf_op jit(solution)/shard_map/all_to_all | solution.py:16
  164.5 4.5 %fusion = bf16[1,2304,512]{1,2,0:T(8,128)(2,1)} fusion(bf16[512,512]{1,0:T(8,128)(2,1)S(1)} %bitcast.42, bf16[512,1,2304]{2,0,1:T(8,128)(2,1)} %param.5), kind=kOutput, calls=%fused_computation.2 | convolution fusion | flops 1209139200 | bytes 5242880 | tf_op jit(solution)/shard_map/dot_general | solution.py:71
  169.0 4.3 %copy.8 = bf16[1,2304,512]{2,1,0:T(8,128)(2,1)} copy(bf16[1,2304,512]{1,2,0:T(8,128)(2,1)} %fusion) | data formatting | bytes 4718592
  (22 shorter events, 0.2 us)
Async XLA Ops:
  0.6 60.5 %copy-start = (bf16[512,1,2304]{2,0,1:T(8,128)(2,1)S(1)}, bf16[512,1,2304]{2,0,1:T(8,128)(2,1)}, u32[]{:S(2)}) copy-start(bf16[512,1,2304]{2,0,1:T(8,128)(2,1)} %param.7) | copy-start | bytes 7077892
  4.6 35.7 %copy-start.7 = (f32[512]{0:T(512)S(1)}, f32[512]{0:T(512)}, u32[]{:S(2)}) copy-start(f32[512]{0:T(512)} %param.8) | copy-start | bytes 6148
  40.3 22.6 %copy-start.4 = (f32[32,512]{1,0:T(8,128)}, f32[32,512]{1,0:T(8,128)S(1)}, u32[]{:S(2)}) copy-start(f32[32,512]{1,0:T(8,128)S(1)} %reduce_sum.27) | copy-start | bytes 196612
  41.2 20.0 %all-to-all-start.1 = ((bf16[16,32,512]{2,1,0:T(8,128)(2,1)}), bf16[16,32,512]{2,1,0:T(8,128)(2,1)S(1)}, u32[]{:S(2)}, u32[]{:S(2)}) async-start(bf16[16,32,512]{2,1,0:T(8,128)(2,1)} %broadcast_in_dim.7), calls=%async_computation.1 | async-start | bytes 1048576 | tf_op jit(solution)/shard_map/all_to_all | solution.py:16
  61.1 8.1 %copy-start.1 = (bf16[16,32,512]{2,1,0:T(8,128)(2,1)}, bf16[16,32,512]{2,1,0:T(8,128)(2,1)S(1)}, u32[]{:S(2)}) copy-start(bf16[16,32,512]{2,1,0:T(8,128)(2,1)S(1)} %all-to-all-done.1) | copy-start | bytes 1572868
  62.9 3.2 %collective-permute-start = (bf16[256,2304]{1,0:T(8,128)(2,1)}, bf16[256,2304]{1,0:T(8,128)(2,1)}, u32[]{:S(2)}, u32[]{:S(2)}) collective-permute-start(bf16[256,2304]{1,0:T(8,128)(2,1)} %convolution_convert_fusion.2), channel_id=1, source_target_pairs={{0,1},{1,0},{2,3},{3,2},{4,5},{5,4},{6,7},{7,6},{8,9},{9,8},{10,11... | collective-permute-start | bytes 3538952 | tf_op jit(solution)/shard_map/ppermute | solution.py:41
  69.2 23.2 %all-to-all-start.2 = ((bf16[8,32,2304]{2,1,0:T(8,128)(2,1)}), bf16[8,32,2304]{2,1,0:T(8,128)(2,1)S(1)}, u32[]{:S(2)}, u32[]{:S(2)}) async-start(bf16[8,32,2304]{2,1,0:T(8,128)(2,1)} %bitcast.5), calls=%async_computation.2 | async-start | bytes 2359296 | tf_op jit(solution)/shard_map/all_to_all | solution.py:46
  116.8 3.0 %copy-start.3 = (bf16[8,32,2304]{2,1,0:T(8,128)(2,1)}, bf16[8,32,2304]{2,1,0:T(8,128)(2,1)S(1)}, u32[]{:S(2)}) copy-start(bf16[8,32,2304]{2,1,0:T(8,128)(2,1)S(1)} %all_to_all.31) | copy-start | bytes 3538948
  116.8 3.0 %collective-permute-start.1 = (bf16[256,2304]{1,0:T(8,128)(2,1)S(1)}, bf16[256,2304]{1,0:T(8,128)(2,1)}, u32[]{:S(2)}, u32[]{:S(2)}) collective-permute-start(bf16[256,2304]{1,0:T(8,128)(2,1)S(1)} %bitcast.39), channel_id=1, source_target_pairs={{0,1},{1,0},{2,3},{3,2},{4,5},{5,4},{6,7},{7,6},{8,9},{9,8},{10,11... | collective-permute-start | bytes 3538952 | tf_op jit(solution)/shard_map/ppermute | solution.py:53
  116.8 26.6 %copy-start.5 = (f32[32,512]{1,0:T(8,128)S(1)}, f32[32,512]{1,0:T(8,128)}, u32[]{:S(2)}) copy-start(f32[32,512]{1,0:T(8,128)} %copy-done.4) | copy-start | bytes 196612
  122.9 26.3 %copy-start.2 = (bf16[16,32,512]{2,1,0:T(8,128)(2,1)S(1)}, bf16[16,32,512]{2,1,0:T(8,128)(2,1)}, u32[]{:S(2)}) copy-start(bf16[16,32,512]{2,1,0:T(8,128)(2,1)} %copy-done.1) | copy-start | bytes 1572868
  143.4 11.2 %copy-start.6 = (f32[32,512]{1,0:T(8,128)}, f32[32,512]{1,0:T(8,128)S(1)}, u32[]{:S(2)}) copy-start(f32[32,512]{1,0:T(8,128)S(1)} %convert_reduce_fusion.1) | copy-start | bytes 196612
  144.3 20.2 %all-to-all-start.5 = ((bf16[16,32,512]{2,1,0:T(8,128)(2,1)}), bf16[16,32,512]{2,1,0:T(8,128)(2,1)S(1)}, u32[]{:S(2)}, u32[]{:S(2)}) async-start(bf16[16,32,512]{2,1,0:T(8,128)(2,1)} %broadcast_in_dim.9), calls=%async_computation.5 | async-start | bytes 1048576 | tf_op jit(solution)/shard_map/all_to_all | solution.py:16

commit v2 on v1

--- a/solution.py
+++ b/solution.py
@@ -3,6 +3,8 @@
 import jax
 import jax.numpy as jnp
 from jax import lax
+from jax.experimental import pallas as pl
+from jax.experimental.pallas import tpu as pltpu
 from jax.sharding import PartitionSpec as P
 
 F32 = jnp.float32
@@ -11,9 +13,41 @@
 CHIP_GROUPS = [list(range(c, 16, 2)) for c in range(2)]
 
 
+Z_UP = [(x * 8 + z, x * 8 + (z + 1) % 8) for x in range(2) for z in range(8)]
+Z_DOWN = [(b, a) for a, b in Z_UP]
+X_NEXT = [(i, (i + 8) % 16) for i in range(16)]
+
+
 def spread(block, axis, groups=None, count=16):
     copies = jnp.broadcast_to(block[None], (count,) + block.shape)
     return lax.all_to_all(copies, axis, 0, 0, axis_index_groups=groups)
+
+
+def matmul_kernel(left_ref, right_ref, out_ref):
+    out_ref[...] = jnp.dot(
+        left_ref[...], right_ref[...], preferred_element_type=F32
+    ).astype(out_ref.dtype)
+
+
+def matmul(left, right, block):
+    rows, depth = left.shape
+    cols = right.shape[1]
+    return pl.pallas_call(
+        matmul_kernel,
+        out_shape=jax.ShapeDtypeStruct((rows, cols), BF16),
+        grid=(rows // block,),
+        in_specs=[
+            pl.BlockSpec((block, depth), lambda i: (i, 0)),
+            pl.BlockSpec((depth, cols), lambda i: (0, 0)),
+        ],
+        out_specs=pl.BlockSpec((block, cols), lambda i: (i, 0)),
+        compiler_params=pltpu.CompilerParams(vmem_limit_bytes=16 * 1024 * 1024),
+        cost_estimate=pl.CostEstimate(
+            flops=2 * rows * depth * cols,
+            bytes_accessed=2 * (rows * depth + depth * cols + rows * cols),
+            transcendentals=0,
+        ),
+    )(left, right)
 
 
 def local(acts, enc_weight, dec_weight, enc_bias, dec_bias):
@@ -29,9 +63,27 @@
     own_half = core * half
     other_half = (1 - core) * half
 
-    partial_pre = jnp.dot(flat, enc, preferred_element_type=F32)
-    parts = lax.all_to_all(partial_pre.reshape(16, rows, local_latents), "layer", 0, 0)
-    own_pre = jnp.sum(parts, axis=0) + enc_bias[None, :]
+    layer_at = lax.axis_index("layer")
+    x_lo = layer_at // 8
+    z = layer_at % 8
+    tall = flat.reshape(2, 8, rows, width)
+
+    def partial(step):
+        block = lax.dynamic_index_in_dim(tall, (z + step) % 8, 1, keepdims=False)
+        return jnp.dot(block.reshape(2 * rows, width), enc, preferred_element_type=F32)
+
+    up, down = partial(4), partial(-3)
+    up, down = lax.ppermute(up, "layer", Z_UP), lax.ppermute(down, "layer", Z_DOWN)
+    up, down = up + partial(3), down + partial(-2)
+    up, down = lax.ppermute(up, "layer", Z_UP), lax.ppermute(down, "layer", Z_DOWN)
+    up, down = up + partial(2), down + partial(-1)
+    up, down = lax.ppermute(up, "layer", Z_UP), lax.ppermute(down, "layer", Z_DOWN)
+    own = partial(0)
+    up = lax.ppermute(up + partial(1), "layer", Z_UP)
+    column = (up + (down + own)).reshape(2, rows, local_latents)
+    kept_column = lax.dynamic_index_in_dim(column, x_lo, 0, keepdims=False)
+    sent_column = lax.dynamic_index_in_dim(column, 1 - x_lo, 0, keepdims=False)
+    own_pre = kept_column + lax.ppermute(sent_column, "layer", X_NEXT) + enc_bias[None, :]
     own_latents = jnp.maximum(own_pre, 0.0).astype(BF16)
     latents = spread(own_latents, "layer").reshape(tokens, local_latents)
 
@@ -68,9 +120,7 @@
     dec_grad = lax.dot_general(
         latents, err, (((0,), (0,)), ((), ())), preferred_element_type=F32
     ).astype(BF16)
-    enc_grad = lax.dot_general(
-        flat, grad_pre, (((0,), (0,)), ((), ())), preferred_element_type=F32
-    ).astype(BF16)
+    enc_grad = matmul(flat.T, grad_pre, 384)
     return (
         latent_grad,
         enc_grad.reshape(layers_here, width, local_latents),

time: 174 us -> 165 us (0.948)
  blocking collectives: 79.3 us -> 43.4 us
  starting transfers between devices: 16.1 us -> 30.7 us
  waiting for transfers between devices: 47.3 us -> 55.7 us
  matrix products: 21.7 us -> 17.2 us
  local copies, waits for them, and re-layouts: 6.1 us -> 10.3 us
  Pallas kernels: 0 us -> 3.72 us
    all_to_all x1 -> x0, blocking collectives: 35.6 us -> none  [local(): lax.all_to_all(partial_pre.reshape(16, rows, local_latents), 'layer', 0, 0)]
    ppermute x0 -> x8, waiting for transfers between devices: none -> 16.2 us  [the longest x3 6.17 us: local(): lax.ppermute(up, 'layer', Z_UP)]
    ppermute x0 -> x8, starting transfers between devices: none -> 10 us  [the longest x3 5.25 us: local(): lax.ppermute(down, 'layer', Z_DOWN)]
    all_to_all x2, waiting for transfers between devices: 24.7 us -> 16.9 us  [spread(): return lax.all_to_all(copies, axis, 0, 0, axis_index_groups=groups)]
    all_to_all x2, starting transfers between devices: 10 us -> 14.6 us  [spread(): return lax.all_to_all(copies, axis, 0, 0, axis_index_groups=groups)]
    dot_general x2 -> x8, matrix products: 8.41 us -> 4.12 us  [partial(): jnp.dot(block.reshape(2 * rows, width), enc, preferred_element_type=F32)]
    pallas_call x0 -> x1, Pallas kernels: none -> 3.72 us  [matmul(): pl.pallas_call(matmul_kernel, out_shape=jax.ShapeDtypeStruct((rows, cols)...]
    unnamed x17 -> x25, local copies, waits for them, and re-layouts: 4.32 us -> 6.64 us
  transfers between devices with their start and end apart: 5 -> 13, of which waited for: 5 -> 12; matrix products, arithmetic and copies ran while one was open for 4% -> 8% of each run, Pallas kernels for 0% -> 0%
where the time goes in v2:
time: 165 us; the launch traced here: 164 us
  waiting for transfers between devices  55.7 us (34%)
  blocking collectives  43.4 us (26%)
  starting transfers between devices  30.7 us (19%)
  matrix products  17.2 us (10%)
  local copies, waits for them, and re-layouts  10.3 us (6%)
  Pallas kernels  3.72 us (2%)
  other arithmetic  2.04 us (1%)
    all_to_all x1, blocking collectives, spread(): return lax.all_to_all(copies, axis, 0, 0, axis_index_groups=groups)  23.2 us
    all_to_all x1, blocking collectives, local(): lax.all_to_all(back.astype(BF16).reshape(16, rows, local_latents), 'layer...  20.3 us
    all_to_all x2, waiting for transfers between devices, spread(): return lax.all_to_all(copies, axis, 0, 0, axis_index_groups=groups)  16.9 us
    all_to_all x1, waiting for transfers between devices, local(): lax.all_to_all(pair.reshape(8, rows, width), 'latent', 0, 0, axis_index_g...  16.4 us
    all_to_all x2, starting transfers between devices, spread(): return lax.all_to_all(copies, axis, 0, 0, axis_index_groups=groups)  14.6 us
    unnamed x25, local copies, waits for them, and re-layouts  6.64 us
    ppermute x3, waiting for transfers between devices, local(): lax.ppermute(up, 'layer', Z_UP)  6.17 us
    all_to_all x1, starting transfers between devices, local(): lax.all_to_all(pair.reshape(8, rows, width), 'latent', 0, 0, axis_index_g...  6.03 us
  transfers between devices with their start and end apart: 13, of which 12 were waited for; matrix products, arithmetic and copies ran while one was open for 8% of the time, Pallas kernels for 0%

profile of v2, /device:TPU:34, one launch (start us, length us, event | category | flops | bytes accessed | tf_op | source)
XLA Modules:
  0.0 164.2 jit_solution(7265103623055144949)
XLA Ops:
  0.8 1.9 %constant_dynamic-slice_fusion = (bf16[2,1,32,2304]{3,2,1,0:T(8,128)(2,1)S(1)}, bf16[2,1,32,2304]{3,2,1,0:T(8,128)(2,1)S(1)}, bf16[2,1,32,2304]{3,2,1,0:T(8,128)...) fusion(bf16[2,8,32,2304]{3,2,1,0:T(8,128)(2,1)} %bitcast.77, ...), kind=kLoop, calls=%fused_computation.44 | loop fusion | bytes 4718624 | tf_op jit(solution)/shard_map/jit(dynamic_index_in_dim)/dynamic_slice | solution.py:72
  3.8 2.0 %collective-permute-start = (f32[64,512]{1,0:T(8,128)S(1)}, f32[64,512]{1,0:T(8,128)S(1)}, u32[]{:S(2)}, u32[]{:S(2)}) collective-permute-start(f32[64,512]{1,0:T(8,128)S(1)} %fusion.20), channel_id=1, source_target_pairs={{0,16},{16,32},{32,48},{48,64},{64,80},{80,96},{96,112},{112,0},{1... | collective-permute-start | bytes 393224 | tf_op jit(solution)/shard_map/ppermute | solution.py:76
  9.7 2.0 %collective-permute-start.1 = (f32[64,512]{1,0:T(8,128)S(1)}, f32[64,512]{1,0:T(8,128)S(1)}, u32[]{:S(2)}, u32[]{:S(2)}) collective-permute-start(f32[64,512]{1,0:T(8,128)S(1)} %fusion.25), channel_id=1, source_target_pairs={{0,16},{16,32},{32,48},{48,64},{64,80},{80,96},{96,112},{112,0},{1... | collective-permute-start | bytes 393224 | tf_op jit(solution)/shard_map/ppermute | solution.py:78
  12.2 2.4 %collective-permute-start.5 = (f32[64,512]{1,0:T(8,128)S(1)}, f32[64,512]{1,0:T(8,128)S(1)}, u32[]{:S(2)}, u32[]{:S(2)}) collective-permute-start(f32[64,512]{1,0:T(8,128)S(1)} %fusion.28), channel_id=1, source_target_pairs={{16,0},{32,16},{48,32},{64,48},{80,64},{96,80},{112,96},{0,112},{1... | collective-permute-start | bytes 393224 | tf_op jit(solution)/shard_map/ppermute | solution.py:78
  14.6 2.3 %collective-permute-done.1 = f32[64,512]{1,0:T(8,128)S(1)} collective-permute-done((f32[64,512]{1,0:T(8,128)S(1)}, f32[64,512]{1,0:T(8,128)S(1)}, u32[]{:S(2)}, u32[]{:S(2)}) %collective-permute-start.1) | collective-permute-done | bytes 131104 | tf_op jit(solution)/shard_map/ppermute | solution.py:78
  18.3 2.7 %collective-permute-start.6 = (f32[64,512]{1,0:T(8,128)S(1)}, f32[64,512]{1,0:T(8,128)S(1)}, u32[]{:S(2)}, u32[]{:S(2)}) collective-permute-start(f32[64,512]{1,0:T(8,128)S(1)} %add.173), channel_id=1, source_target_pairs={{16,0},{32,16},{48,32},{64,48},{80,64},{96,80},{112,96},{0,112},{1... | collective-permute-start | bytes 393224 | tf_op jit(solution)/shard_map/ppermute | solution.py:80
  20.9 2.3 %collective-permute-done.2 = f32[64,512]{1,0:T(8,128)S(1)} collective-permute-done((f32[64,512]{1,0:T(8,128)S(1)}, f32[64,512]{1,0:T(8,128)S(1)}, u32[]{:S(2)}, u32[]{:S(2)}) %collective-permute-start.2) | collective-permute-done | bytes 131104 | tf_op jit(solution)/shard_map/ppermute | solution.py:80
  24.5 5.0 %collective-permute-done.3 = f32[64,512]{1,0:T(8,128)S(1)} collective-permute-done((f32[64,512]{1,0:T(8,128)S(1)}, f32[64,512]{1,0:T(8,128)S(1)}, u32[]{:S(2)}, u32[]{:S(2)}) %collective-permute-start.3) | collective-permute-done | bytes 131104 | tf_op jit(solution)/shard_map/ppermute | solution.py:82
  30.2 3.7 %collective-permute-done.7 = f32[32,512]{1,0:T(8,128)S(1)} collective-permute-done((f32[32,512]{1,0:T(8,128)S(1)}, f32[32,512]{1,0:T(8,128)S(1)}, u32[]{:S(2)}, u32[]{:S(2)}) %collective-permute-start.7) | collective-permute-done | bytes 65568 | tf_op jit(solution)/shard_map/ppermute | solution.py:86
  34.8 9.7 %all-to-all-start = ((bf16[16,32,512]{2,1,0:T(8,128)(2,1)}), bf16[16,32,512]{2,1,0:T(8,128)(2,1)S(1)}, u32[]{:S(2)}, u32[]{:S(2)}) async-start(bf16[16,32,512]{2,1,0:T(8,128)(2,1)} %broadcast_in_dim.7), calls=%async_computation | async-start | bytes 1048576 | tf_op jit(solution)/shard_map/all_to_all | solution.py:23
  44.5 11.2 %all-to-all-done = bf16[16,32,512]{2,1,0:T(8,128)(2,1)S(1)} async-done(((bf16[16,32,512]{2,1,0:T(8,128)(2,1)}), bf16[16,32,512]{2,1,0:T(8,128)(2,1)S(1)}, u32[]{:S(2)}, u32[]{:S(2)}) %all-to-all-start) | async-done | bytes 524320 | tf_op jit(solution)/shard_map/all_to_all | solution.py:23
  57.5 3.2 %collective-permute-done.8 = bf16[256,2304]{1,0:T(8,128)(2,1)} collective-permute-done((bf16[256,2304]{1,0:T(8,128)(2,1)}, bf16[256,2304]{1,0:T(8,128)(2,1)}, u32[]{:S(2)}, u32[]{:S(2)}) %collective-permute-start.8) | collective-permute-done | bytes 1179680 | tf_op jit(solution)/shard_map/ppermute | solution.py:93
  60.7 3.1 %add_convert_fusion = bf16[256,2304]{1,0:T(8,128)(2,1)} fusion(bf16[256,2304]{1,0:T(8,128)(2,1)} %collective-permute-done.8, bf16[512,1,2304]{2,0,1:T(8,128)(2,1)S(1)} %copy-done, bf16[512,512]{1,0:T(8,128)(2,1)S(1)} %bitcast.80, s32[]{:T(128)S(6)} %select_n.125), kind=kOutput, calls=%fused_computation.26 | convolution fusion | flops 605749248 | bytes 4980740 | tf_op jit(solution)/shard_map/dot_general | solution.py:94
  63.8 6.0 %all-to-all-start.1 = ((bf16[8,32,2304]{2,1,0:T(8,128)(2,1)}), bf16[8,32,2304]{2,1,0:T(8,128)(2,1)S(1)}, u32[]{:S(2)}, u32[]{:S(2)}) async-start(bf16[8,32,2304]{2,1,0:T(8,128)(2,1)} %bitcast.15), calls=%async_computation.1 | async-start | bytes 2359296 | tf_op jit(solution)/shard_map/all_to_all | solution.py:98
  70.5 16.4 %all-to-all-done.1 = bf16[8,32,2304]{2,1,0:T(8,128)(2,1)S(1)} async-done(((bf16[8,32,2304]{2,1,0:T(8,128)(2,1)}), bf16[8,32,2304]{2,1,0:T(8,128)(2,1)S(1)}, u32[]{:S(2)}, u32[]{:S(2)}) %all-to-all-start.1) | async-done | bytes 1179680 | tf_op jit(solution)/shard_map/all_to_all | solution.py:98
  88.2 23.2 %all_to_all.25 = bf16[8,32,2304]{2,1,0:T(8,128)(2,1)S(1)} all-to-all(bf16[8,32,2304]{2,1,0:T(8,128)(2,1)S(1)} %broadcast_in_dim.8), channel_id=1, replica_groups={{0,2,4,6,8,10,12,14},{1,3,5,7,9,11,13,15},{16,18,20,22,24,26,28,30},{17..., dimensions={0} | all-to-all | bytes 2359296 | tf_op jit(solution)/shard_map/all_to_all | solution.py:23
  111.4 3.0 %collective-permute-done.9 = bf16[256,2304]{1,0:T(8,128)(2,1)} collective-permute-done((bf16[256,2304]{1,0:T(8,128)(2,1)S(1)}, bf16[256,2304]{1,0:T(8,128)(2,1)}, u32[]{:S(2)}, u32[]{:S(2)}) %collective-permute-start.9) | collective-permute-done | bytes 1179680 | tf_op jit(solution)/shard_map/ppermute | solution.py:105
  114.4 3.0 %fusion.22 = bf16[512,512]{1,0:T(8,128)(2,1)S(1)} fusion(bf16[512,1,2304]{2,0,1:T(8,128)(2,1)S(1)} %copy-done, bf16[256,2304]{1,0:T(8,128)(2,1)} %collective-permute-done.9, bf16[256,2304]{1,0:T(8,128)(2,1)S(1)} %bitcast.83, pred[]{:T(512)S(6)} %eq.14), kind=kOutput, calls=%fused_computation.27 | convolution fusion | flops 1218838528 | bytes 5242881 | tf_op jit(solution)/shard_map/dot_general | solution.py:112
  117.4 20.3 %all_to_all.26 = bf16[16,32,512]{2,1,0:T(8,128)(2,1)S(1)} all-to-all(bf16[16,32,512]{2,1,0:T(8,128)(2,1)S(1)} %bitcast.96), channel_id=1, replica_groups=mesh['layer'=16,'latent'=16] {'layer'}, dimensions={0} | all-to-all | bytes 1048576 | tf_op jit(solution)/shard_map/all_to_all | solution.py:113
  138.7 4.9 %all-to-all-start.4 = ((bf16[16,32,512]{2,1,0:T(8,128)(2,1)}), bf16[16,32,512]{2,1,0:T(8,128)(2,1)S(1)}, u32[]{:S(2)}, u32[]{:S(2)}) async-start(bf16[16,32,512]{2,1,0:T(8,128)(2,1)} %broadcast_in_dim.9), calls=%async_computation.4 | async-start | bytes 1048576 | tf_op jit(solution)/shard_map/all_to_all | solution.py:23
  143.6 4.3 %copy.8 = bf16[512,1,2304]{0,2,1:T(8,128)(2,1)} copy(bf16[512,1,2304]{2,0,1:T(8,128)(2,1)} %param.5) | data formatting | bytes 4718592 | tf_op args[0]
  147.9 5.2 %fusion = bf16[512,1,2304]{2,0,1:T(8,128)(2,1)} fusion(bf16[512,512]{1,0:T(8,128)(2,1)S(1)} %bitcast.81, bf16[256,2304]{1,0:T(8,128)(2,1)} %collective-permute-done.9, bf16[256,2304]{1,0:T(8,128)(2,1)} %bitcast.84, pred[]{:T(512)S(6)} %eq.14), kind=kOutput, calls=%fused_computation.1 | convolution fusion | flops 1219756032 | bytes 5242881 | tf_op jit(solution)/shard_map/dot_general | solution.py:120
  153.1 5.7 %all-to-all-done.4 = bf16[16,32,512]{2,1,0:T(8,128)(2,1)S(1)} async-done(((bf16[16,32,512]{2,1,0:T(8,128)(2,1)}), bf16[16,32,512]{2,1,0:T(8,128)(2,1)S(1)}, u32[]{:S(2)}, u32[]{:S(2)}) %all-to-all-start.4) | async-done | bytes 524320 | tf_op jit(solution)/shard_map/all_to_all | solution.py:23
  160.5 3.7 %shard_map.79 = bf16[2304,512]{1,0:T(8,128)(2,1)} custom-call(bf16[2304,512]{1,0:T(8,128)(2,1)S(1)} %bitcast.75, bf16[512,512]{1,0:T(8,128)(2,1)S(1)} %bitcast.76), custom_call_target="tpu_custom_call" | custom-call | flops 1207959552 | bytes 5242880 | tf_op jit(solution)/shard_map/pallas_call | solution.py:35
  (57 shorter events, 15.9 us)
Async XLA Ops:
  0.6 55.1 %copy-start = (bf16[512,1,2304]{2,0,1:T(8,128)(2,1)S(1)}, bf16[512,1,2304]{2,0,1:T(8,128)(2,1)}, u32[]{:S(2)}) copy-start(bf16[512,1,2304]{2,0,1:T(8,128)(2,1)} %param.7) | copy-start | bytes 7077892
  0.8 2.5 %copy-start.2 = (bf16[1,2304,512]{2,1,0:T(8,128)(2,1)S(1)}, bf16[1,2304,512]{2,1,0:T(8,128)(2,1)}, u32[]{:S(2)}) copy-start(bf16[1,2304,512]{2,1,0:T(8,128)(2,1)} %param.6) | copy-start | bytes 7077892
  3.8 5.3 %collective-permute-start = (f32[64,512]{1,0:T(8,128)S(1)}, f32[64,512]{1,0:T(8,128)S(1)}, u32[]{:S(2)}, u32[]{:S(2)}) collective-permute-start(f32[64,512]{1,0:T(8,128)S(1)} %fusion.20), channel_id=1, source_target_pairs={{0,16},{16,32},{32,48},{48,64},{64,80},{80,96},{96,112},{112,0},{1... | collective-permute-start | bytes 393224 | tf_op jit(solution)/shard_map/ppermute | solution.py:76
  6.4 5.3 %collective-permute-start.4 = (f32[64,512]{1,0:T(8,128)S(1)}, f32[64,512]{1,0:T(8,128)S(1)}, u32[]{:S(2)}, u32[]{:S(2)}) collective-permute-start(f32[64,512]{1,0:T(8,128)S(1)} %fusion.12), channel_id=1, source_target_pairs={{16,0},{32,16},{48,32},{64,48},{80,64},{96,80},{112,96},{0,112},{1... | collective-permute-start | bytes 393224 | tf_op jit(solution)/shard_map/ppermute | solution.py:76
  9.7 7.2 %collective-permute-start.1 = (f32[64,512]{1,0:T(8,128)S(1)}, f32[64,512]{1,0:T(8,128)S(1)}, u32[]{:S(2)}, u32[]{:S(2)}) collective-permute-start(f32[64,512]{1,0:T(8,128)S(1)} %fusion.25), channel_id=1, source_target_pairs={{0,16},{16,32},{32,48},{48,64},{64,80},{80,96},{96,112},{112,0},{1... | collective-permute-start | bytes 393224 | tf_op jit(solution)/shard_map/ppermute | solution.py:78
  12.2 6.0 %collective-permute-start.5 = (f32[64,512]{1,0:T(8,128)S(1)}, f32[64,512]{1,0:T(8,128)S(1)}, u32[]{:S(2)}, u32[]{:S(2)}) collective-permute-start(f32[64,512]{1,0:T(8,128)S(1)} %fusion.28), channel_id=1, source_target_pairs={{16,0},{32,16},{48,32},{64,48},{80,64},{96,80},{112,96},{0,112},{1... | collective-permute-start | bytes 393224 | tf_op jit(solution)/shard_map/ppermute | solution.py:78
  17.0 6.3 %collective-permute-start.2 = (f32[64,512]{1,0:T(8,128)S(1)}, f32[64,512]{1,0:T(8,128)S(1)}, u32[]{:S(2)}, u32[]{:S(2)}) collective-permute-start(f32[64,512]{1,0:T(8,128)S(1)} %add.158), channel_id=1, source_target_pairs={{0,16},{16,32},{32,48},{48,64},{64,80},{80,96},{96,112},{112,0},{1... | collective-permute-start | bytes 393224 | tf_op jit(solution)/shard_map/ppermute | solution.py:80
  17.6 16.3 %copy-start.11 = (f32[512]{0:T(512)S(1)}, f32[512]{0:T(512)}, u32[]{:S(2)}) copy-start(f32[512]{0:T(512)} %param.8) | copy-start | bytes 6148
  18.3 6.3 %collective-permute-start.6 = (f32[64,512]{1,0:T(8,128)S(1)}, f32[64,512]{1,0:T(8,128)S(1)}, u32[]{:S(2)}, u32[]{:S(2)}) collective-permute-start(f32[64,512]{1,0:T(8,128)S(1)} %add.173), channel_id=1, source_target_pairs={{16,0},{32,16},{48,32},{64,48},{80,64},{96,80},{112,96},{0,112},{1... | collective-permute-start | bytes 393224 | tf_op jit(solution)/shard_map/ppermute | solution.py:80
  23.2 6.3 %collective-permute-start.3 = (f32[64,512]{1,0:T(8,128)S(1)}, f32[64,512]{1,0:T(8,128)S(1)}, u32[]{:S(2)}, u32[]{:S(2)}) collective-permute-start(f32[64,512]{1,0:T(8,128)S(1)} %add.162), channel_id=1, source_target_pairs={{0,16},{16,32},{32,48},{48,64},{64,80},{80,96},{96,112},{112,0},{1... | collective-permute-start | bytes 393224 | tf_op jit(solution)/shard_map/ppermute | solution.py:82
  29.5 5.3 %copy-start.6 = (f32[64,512]{1,0:T(8,128)}, f32[64,512]{1,0:T(8,128)S(1)}, u32[]{:S(2)}) copy-start(f32[64,512]{1,0:T(8,128)S(1)} %add_add_fusion) | copy-start | bytes 393220
  29.6 4.4 %collective-permute-start.7 = (f32[32,512]{1,0:T(8,128)S(1)}, f32[32,512]{1,0:T(8,128)S(1)}, u32[]{:S(2)}, u32[]{:S(2)}) collective-permute-start(f32[32,512]{1,0:T(8,128)S(1)} %dynamic-slice_bitcast_fusion), channel_id=1, source_target_pairs={{0,128},{16,144},{32,160},{48,176},{64,192},{80,208},{96,224},{112... | collective-permute-start | bytes 196616 | tf_op jit(solution)/shard_map/ppermute | solution.py:86
  34.8 20.9 %all-to-all-start = ((bf16[16,32,512]{2,1,0:T(8,128)(2,1)}), bf16[16,32,512]{2,1,0:T(8,128)(2,1)S(1)}, u32[]{:S(2)}, u32[]{:S(2)}) async-start(bf16[16,32,512]{2,1,0:T(8,128)(2,1)} %broadcast_in_dim.7), calls=%async_computation | async-start | bytes 1048576 | tf_op jit(solution)/shard_map/all_to_all | solution.py:23
  55.7 8.1 %copy-start.3 = (bf16[16,32,512]{2,1,0:T(8,128)(2,1)}, bf16[16,32,512]{2,1,0:T(8,128)(2,1)S(1)}, u32[]{:S(2)}) copy-start(bf16[16,32,512]{2,1,0:T(8,128)(2,1)S(1)} %all-to-all-done) | copy-start | bytes 1572868
  57.5 3.2 %collective-permute-start.8 = (bf16[256,2304]{1,0:T(8,128)(2,1)}, bf16[256,2304]{1,0:T(8,128)(2,1)}, u32[]{:S(2)}, u32[]{:S(2)}) collective-permute-start(bf16[256,2304]{1,0:T(8,128)(2,1)} %convolution_convert_fusion.1), channel_id=1, source_target_pairs={{0,1},{1,0},{2,3},{3,2},{4,5},{5,4},{6,7},{7,6},{8,9},{9,8},{10,11... | collective-permute-start | bytes 3538952 | tf_op jit(solution)/shard_map/ppermute | solution.py:93
  63.8 23.2 %all-to-all-start.1 = ((bf16[8,32,2304]{2,1,0:T(8,128)(2,1)}), bf16[8,32,2304]{2,1,0:T(8,128)(2,1)S(1)}, u32[]{:S(2)}, u32[]{:S(2)}) async-start(bf16[8,32,2304]{2,1,0:T(8,128)(2,1)} %bitcast.15), calls=%async_computation.1 | async-start | bytes 2359296 | tf_op jit(solution)/shard_map/all_to_all | solution.py:98
  111.4 6.0 %copy-start.5 = (bf16[8,32,2304]{2,1,0:T(8,128)(2,1)}, bf16[8,32,2304]{2,1,0:T(8,128)(2,1)S(1)}, u32[]{:S(2)}) copy-start(bf16[8,32,2304]{2,1,0:T(8,128)(2,1)S(1)} %all_to_all.25) | copy-start | bytes 3538948
  111.4 3.0 %collective-permute-start.9 = (bf16[256,2304]{1,0:T(8,128)(2,1)S(1)}, bf16[256,2304]{1,0:T(8,128)(2,1)}, u32[]{:S(2)}, u32[]{:S(2)}) collective-permute-start(bf16[256,2304]{1,0:T(8,128)(2,1)S(1)} %bitcast.82), channel_id=1, source_target_pairs={{0,1},{1,0},{2,3},{3,2},{4,5},{5,4},{6,7},{7,6},{8,9},{9,8},{10,11... | collective-permute-start | bytes 3538952 | tf_op jit(solution)/shard_map/ppermute | solution.py:105
  111.4 26.4 %copy-start.7 = (f32[64,512]{1,0:T(8,128)S(1)}, f32[64,512]{1,0:T(8,128)}, u32[]{:S(2)}) copy-start(f32[64,512]{1,0:T(8,128)} %copy-done.6) | copy-start | bytes 393220
  111.4 26.4 %copy-start.10 = (f32[32,512]{1,0:T(8,128)S(1)}, f32[32,512]{1,0:T(8,128)}, u32[]{:S(2)}) copy-start(f32[32,512]{1,0:T(8,128)} %copy-done.9) | copy-start | bytes 196612
  137.8 10.1 %copy-start.8 = (f32[32,512]{1,0:T(8,128)}, f32[32,512]{1,0:T(8,128)S(1)}, u32[]{:S(2)}) copy-start(f32[32,512]{1,0:T(8,128)S(1)} %convert_reduce_fusion.1) | copy-start | bytes 196612
  138.7 20.2 %all-to-all-start.4 = ((bf16[16,32,512]{2,1,0:T(8,128)(2,1)}), bf16[16,32,512]{2,1,0:T(8,128)(2,1)S(1)}, u32[]{:S(2)}, u32[]{:S(2)}) async-start(bf16[16,32,512]{2,1,0:T(8,128)(2,1)} %broadcast_in_dim.9), calls=%async_computation.4 | async-start | bytes 1048576 | tf_op jit(solution)/shard_map/all_to_all | solution.py:23
  143.6 4.3 %copy-start.4 = (bf16[16,32,512]{2,1,0:T(8,128)(2,1)S(1)}, bf16[16,32,512]{2,1,0:T(8,128)(2,1)}, u32[]{:S(2)}) copy-start(bf16[16,32,512]{2,1,0:T(8,128)(2,1)} %copy-done.3) | copy-start | bytes 1572868
  158.8 1.7 %copy-start.1 = (bf16[512,1,2304]{0,2,1:T(8,128)(2,1)S(1)}, bf16[512,1,2304]{0,2,1:T(8,128)(2,1)}, u32[]{:S(2)}) copy-start(bf16[512,1,2304]{0,2,1:T(8,128)(2,1)} %copy.8) | copy-start | bytes 7077892
  (1 other events, 0.9 us)

commit v3 on v2

v3 whole, which is shorter than its diff:
```python
import functools
import math

import jax
import jax.numpy as jnp
from jax import lax
from jax.experimental import pallas as pl
from jax.experimental.pallas import tpu as pltpu
from jax.sharding import PartitionSpec as P

F32 = jnp.float32
BF16 = jnp.bfloat16
CORE_SWAP = [(i, i ^ 1) for i in range(16)]
CHIP_GROUPS = [list(range(c, 16, 2)) for c in range(2)]


Z_UP = [(x * 8 + z, x * 8 + (z + 1) % 8) for x in range(2) for z in range(8)]
Z_DOWN = [(b, a) for a, b in Z_UP]
X_NEXT = [(i, (i + 8) % 16) for i in range(16)]


def spread(block, axis, groups=None, count=16):
    copies = jnp.broadcast_to(block[None], (count,) + block.shape)
    return lax.all_to_all(copies, axis, 0, 0, axis_index_groups=groups)


SMALL = pl.BlockSpec(memory_space=pltpu.SMEM)
LARGE = pl.BlockSpec(memory_space=pl.ANY)
STORED = pl.BlockSpec(memory_space=pltpu.HBM)
NT = (((1,), (1,)), ((), ()))
PIECES = 3


def shape(dims, dtype):
    return jax.ShapeDtypeStruct(dims, dtype)


def whole(like):
    if like.shape == (1,):
        return SMALL
    return pl.BlockSpec(like.shape, lambda i: (0,) * len(like.shape))


def simple(kernel, out_shape, flops, moved, *operands):
    specs = [whole(operand) for operand in operands]
    return call(kernel, out_shape, whole(out_shape), specs, [], flops, moved, *operands)


def call(kernel, out_shape, out_spec, specs, scratch, flops, moved, *operands):
    return pl.pallas_call(
        kernel,
        out_shape=out_shape,
        grid=(1,),
        in_specs=specs,
        out_specs=out_spec,
        scratch_shapes=scratch,
        compiler_params=pltpu.CompilerParams(vmem_limit_bytes=20 * 1024 * 1024),
        cost_estimate=pl.CostEstimate(flops=flops, bytes_accessed=moved, transcendentals=0),
    )(*operands)


def error_kernel(shares_ref, bias_ref, acts_ref, copies_ref, *, scale):
    recon = shares_ref[0].astype(F32)
    for i in range(1, shares_ref.shape[0]):
        recon += shares_ref[i].astype(F32)
    err = (recon + bias_ref[...] - acts_ref[...].astype(F32)) / scale
    err = err.astype(BF16)
    for i in range(copies_ref.shape[0]):
        copies_ref[i] = err


def half_of(ref, which):
    rows = ref.shape[0] // 2
    return ref[pl.ds(pl.multiple_of(which * rows, rows), rows), :]


def send_kernel(core_ref, latents_ref, dec_ref, out_ref):
    left = half_of(latents_ref, 1 - core_ref[0])
    out_ref[...] = jnp.dot(left, dec_ref[...], preferred_element_type=F32).astype(BF16)


def keep_kernel(core_ref, latents_ref, dec_ref, received_ref, out_ref):
    left = half_of(latents_ref, core_ref[0])
    total = jnp.dot(left, dec_ref[...], preferred_element_type=F32)
    out_ref[...] = (total + received_ref[...].astype(F32)).astype(BF16)


def back_own_kernel(err_ref, dec_ref, out_ref):
    out_ref[...] = lax.dot_general(
        err_ref[...], dec_ref[...], NT, preferred_element_type=F32
    ).astype(BF16)


def back_kernel(core_ref, err_ref, dec_ref, own_ref, out_ref):
    half = err_ref.shape[0]
    core = core_ref[0]
    other = lax.dot_general(err_ref[...], dec_ref[...], NT, preferred_element_type=F32)
    out_ref[pl.ds(pl.multiple_of(core * half, half), half), :] = own_ref[...]
    out_ref[pl.ds(pl.multiple_of((1 - core) * half, half), half), :] = other.astype(BF16)


def enc_kernel(acts_ref, grad_ref, out_ref, acts_buf, out_buf, sems):
    step = acts_ref.shape[0] // PIECES
    rows = [slice(i * step, (i + 1) * step) for i in range(PIECES)]
    loads = [
        pltpu.make_async_copy(acts_ref.at[r], acts_buf.at[r], sems.at[0, i])
        for i, r in enumerate(rows)
    ]
    for load in loads:
        load.start()
    grad = grad_ref[...]
    stores = []
    for i, r in enumerate(rows):
        loads[i].wait()
        out_buf[r] = jnp.dot(acts_buf[r], grad, preferred_element_type=F32).astype(BF16)
        stores.append(pltpu.make_async_copy(out_buf.at[r], out_ref.at[r], sems.at[1, i]))
        stores[-1].start()
    for store in stores:
        store.wait()


def local(acts, enc_weight, dec_weight, enc_bias, dec_bias):
    tokens, layers_here, width = acts.shape
    local_latents = enc_weight.shape[2]
    flat = acts.reshape(tokens, width)
    enc = enc_weight.reshape(width, local_latents)
    dec = dec_weight.reshape(local_latents, width)
    rows = tokens // 16
    half = tokens // 2
    core = lax.axis_index("latent") % 2
    chip = lax.axis_index("latent") // 2
    core_at = core.reshape(1)
    own_half = core * half
    other_half = (1 - core) * half

    layer_at = lax.axis_index("layer")
    x_lo = layer_at // 8
    z = layer_at % 8
    tall = flat.reshape(2, 8, rows, width)

    def partial(step):
        block = lax.dynamic_index_in_dim(tall, (z + step) % 8, 1, keepdims=False)
        return jnp.dot(block.reshape(2 * rows, width), enc, preferred_element_type=F32)

    up, down = partial(4), partial(-3)
    up, down, tall = lax.optimization_barrier((up, down, tall))
    up, down = lax.ppermute(up, "layer", Z_UP), lax.ppermute(down, "layer", Z_DOWN)
    up, down = up + partial(3), down + partial(-2)
    up, down = lax.ppermute(up, "layer", Z_UP), lax.ppermute(down, "layer", Z_DOWN)
    up, down = up + partial(2), down + partial(-1)
    up, down = lax.ppermute(up, "layer", Z_UP), lax.ppermute(down, "layer", Z_DOWN)
    own = partial(0)
    up = lax.ppermute(up + partial(1), "layer", Z_UP)
    column = (up + (down + own)).reshape(2, rows, local_latents)
    kept_column = lax.dynamic_index_in_dim(column, x_lo, 0, keepdims=False)
    sent_column = lax.dynamic_index_in_dim(column, 1 - x_lo, 0, keepdims=False)
    own_pre = kept_column + lax.ppermute(sent_column, "layer", X_NEXT) + enc_bias[None, :]
    own_latents = jnp.maximum(own_pre, 0.0).astype(BF16)
    latents = spread(own_latents, "layer").reshape(tokens, local_latents)

    acts_rows = lax.dynamic_slice_in_dim(flat, own_half + chip * rows, rows, 0)
    latents, acts_t, acts_rows = lax.optimization_barrier((latents, flat.T, acts_rows))
    flops = 2 * half * local_latents * width
    moved = 2 * (local_latents + half) * width
    halves = shape((half, width), BF16)
    send = simple(send_kernel, halves, flops, moved, core_at, latents, dec)
    received = lax.ppermute(send, "latent", CORE_SWAP)
    chip_sum = simple(keep_kernel, halves, flops, moved, core_at, latents, dec, received)
    shares = lax.all_to_all(
        chip_sum.reshape(8, rows, width), "latent", 0, 0, axis_index_groups=CHIP_GROUPS
    )
    copies = shape((8, rows, width), BF16)
    err_copies = simple(
        functools.partial(error_kernel, scale=math.sqrt(tokens)),
        copies,
        12 * rows * width,
        36 * rows * width,
        shares,
        dec_bias,
        acts_rows,
    )
    err_own = lax.all_to_all(err_copies, "latent", 0, 0, axis_index_groups=CHIP_GROUPS)
    err_own = err_own.reshape(half, width)

    err_other = lax.ppermute(err_own, "latent", CORE_SWAP)
    back = simple(
        back_own_kernel, shape((half, local_latents), BF16), flops, moved, err_own, dec
    )
    back = simple(
        back_kernel,
        shape((tokens, local_latents), BF16),
        flops,
        moved,
        core_at,
        err_other,
        dec,
        back,
    )
    err = jnp.where(
        core == 0,
        jnp.concatenate([err_own, err_other], 0),
        jnp.concatenate([err_other, err_own], 0),
    )
    back_parts = lax.all_to_all(
        back.reshape(16, rows, local_latents), "layer", 0, 0
    )
    latent_grad = jnp.sum(back_parts.astype(F32), axis=0)
    own_grad_pre = jnp.where(own_pre > 0, latent_grad, 0.0).astype(BF16)
    latents_late, err_late, latent_grad = lax.optimization_barrier((latents, err, latent_grad))
    dec_grad = lax.dot_general(
        latents_late, err_late, (((0,), (0,)), ((), ())), preferred_element_type=F32
    ).astype(BF16)
    grad_pre = spread(own_grad_pre, "layer").reshape(tokens, local_latents)
    enc_grad = call(
        enc_kernel,
        shape((width, local_latents), BF16),
        STORED,
        [LARGE, whole(grad_pre)],
        [
            pltpu.VMEM((width, tokens), BF16),
            pltpu.VMEM((width, local_latents), BF16),
            pltpu.SemaphoreType.DMA((2, PIECES)),
        ],
        2 * tokens * width * local_latents,
        3 * moved,
        acts_t,
        grad_pre,
    )
    return (
        latent_grad,
        enc_grad.reshape(layers_here, width, local_latents),
        dec_grad.reshape(local_latents, layers_here, width),
    )


def solution(mesh):
    in_specs = (
        P(None, "layer", None),
        P("layer", None, "latent"),
        P("latent", "layer", None),
        P("latent"),
        P("layer", None),
    )
    out_specs = (P("layer", "latent"), P("layer", None, "latent"), P("latent", "layer", None))
    return jax.shard_map(local, mesh=mesh, in_specs=in_specs, out_specs=out_specs, check_vma=False)
```

time: 165 us -> 160 us (0.970)
  blocking collectives: 43.4 us -> 65.8 us
  waiting for transfers between devices: 55.7 us -> 39.9 us
  matrix products: 17.2 us -> 6.97 us
  starting transfers between devices: 30.7 us -> 21.4 us
  local copies, waits for them, and re-layouts: 10.3 us -> 14.4 us
  Pallas kernels: 3.72 us -> 7.25 us
    all_to_all x2 -> x3, blocking collectives: 43.4 us -> 65.8 us  [the longest x1 24.7 us: local(): lax.all_to_all(chip_sum.reshape(8, rows, width), 'latent', 0, 0, axis_ind...]
    all_to_all x1 -> x0, waiting for transfers between devices: 16.4 us -> none  [local(): lax.all_to_all(pair.reshape(8, rows, width), 'latent', 0, 0, axis_index_g...]
    dot_general x4 -> x1, matrix products: 13.1 us -> 2.84 us  [local(): lax.dot_general(latents_late, err_late, (((0,), (0,)), ((), ())), preferr...]
    all_to_all x1 -> x0, starting transfers between devices: 6.03 us -> none  [local(): lax.all_to_all(pair.reshape(8, rows, width), 'latent', 0, 0, axis_index_g...]
    pallas_call x1 -> x6, Pallas kernels: 3.72 us -> 7.25 us  [call(): pl.pallas_call(kernel, out_shape=out_shape, grid=(1,), in_specs=specs, ou...]
    ppermute x3, waiting for transfers between devices: 6.17 us -> 9.16 us  [local(): lax.ppermute(up, 'layer', Z_UP)]
    all_to_all x2, starting transfers between devices: 14.6 us -> 12 us  [spread(): return lax.all_to_all(copies, axis, 0, 0, axis_index_groups=groups)]
    unnamed x25 -> x29, local copies, waits for them, and re-layouts: 6.64 us -> 8.97 us
  transfers between devices with their start and end apart: 13 -> 12, of which waited for: 12 -> 9; matrix products, arithmetic and copies ran while one was open for 8% -> 9% of each run, Pallas kernels for 0% -> 1%
where the time goes in v3:
time: 160 us; the launch traced here: 159 us
  blocking collectives  65.8 us (41%)
  waiting for transfers between devices  39.9 us (25%)
  starting transfers between devices  21.4 us (13%)
  local copies, waits for them, and re-layouts  14.4 us (9%)
  Pallas kernels  7.25 us (5%)
  matrix products  6.97 us (4%)
  other arithmetic  2.16 us (1%)
    all_to_all x1, blocking collectives, local(): lax.all_to_all(chip_sum.reshape(8, rows, width), 'latent', 0, 0, axis_ind...  24.7 us
    all_to_all x1, blocking collectives, local(): lax.all_to_all(err_copies, 'latent', 0, 0, axis_index_groups=CHIP_GROUPS)  20.8 us
    all_to_all x1, blocking collectives, local(): lax.all_to_all(back.reshape(16, rows, local_latents), 'layer', 0, 0)  20.3 us
    all_to_all x2, waiting for transfers between devices, spread(): return lax.all_to_all(copies, axis, 0, 0, axis_index_groups=groups)  16.5 us
    all_to_all x2, starting transfers between devices, spread(): return lax.all_to_all(copies, axis, 0, 0, axis_index_groups=groups)  12 us
    ppermute x3, waiting for transfers between devices, local(): lax.ppermute(up, 'layer', Z_UP)  9.16 us
    unnamed x29, local copies, waits for them, and re-layouts  8.97 us
    pallas_call x6, Pallas kernels, call(): pl.pallas_call(kernel, out_shape=out_shape, grid=(1,), in_specs=specs, ou...  7.25 us
  transfers between devices with their start and end apart: 12, of which 9 were waited for; matrix products, arithmetic and copies ran while one was open for 9% of the time, Pallas kernels for 1%

profile of v3, /device:TPU:34, one launch (start us, length us, event | category | flops | bytes accessed | tf_op | source)
XLA Modules:
  0.0 159.1 jit_solution(16800429390246537026)
XLA Ops:
  3.7 1.9 %collective-permute-start = (f32[64,512]{1,0:T(8,128)S(1)}, f32[64,512]{1,0:T(8,128)S(1)}, u32[]{:S(2)}, u32[]{:S(2)}) collective-permute-start(f32[64,512]{1,0:T(8,128)S(1)} %fusion.15), channel_id=1, source_target_pairs={{0,16},{16,32},{32,48},{48,64},{64,80},{80,96},{96,112},{112,0},{1... | collective-permute-start | bytes 393224 | tf_op jit(solution)/shard_map/ppermute | solution.py:147
  5.6 1.6 constant_dynamic-slice_fusion
  8.2 4.6 %collective-permute-done = f32[64,512]{1,0:T(8,128)S(1)} collective-permute-done((f32[64,512]{1,0:T(8,128)S(1)}, f32[64,512]{1,0:T(8,128)S(1)}, u32[]{:S(2)}, u32[]{:S(2)}) %collective-permute-start) | collective-permute-done | bytes 131104 | tf_op jit(solution)/shard_map/ppermute | solution.py:147
  13.9 3.0 %collective-permute-start.5 = (f32[64,512]{1,0:T(8,128)S(1)}, f32[64,512]{1,0:T(8,128)S(1)}, u32[]{:S(2)}, u32[]{:S(2)}) collective-permute-start(f32[64,512]{1,0:T(8,128)S(1)} %fusion.20), channel_id=1, source_target_pairs={{16,0},{32,16},{48,32},{64,48},{80,64},{96,80},{112,96},{0,112},{1... | collective-permute-start | bytes 393224 | tf_op jit(solution)/shard_map/ppermute | solution.py:149
  17.0 2.3 %collective-permute-done.1 = f32[64,512]{1,0:T(8,128)S(1)} collective-permute-done((f32[64,512]{1,0:T(8,128)S(1)}, f32[64,512]{1,0:T(8,128)S(1)}, u32[]{:S(2)}, u32[]{:S(2)}) %collective-permute-start.1) | collective-permute-done | bytes 131104 | tf_op jit(solution)/shard_map/ppermute | solution.py:149
  20.0 3.3 %collective-permute-start.6 = (f32[64,512]{1,0:T(8,128)S(1)}, f32[64,512]{1,0:T(8,128)S(1)}, u32[]{:S(2)}, u32[]{:S(2)}) collective-permute-start(f32[64,512]{1,0:T(8,128)S(1)} %add.151), channel_id=1, source_target_pairs={{16,0},{32,16},{48,32},{64,48},{80,64},{96,80},{112,96},{0,112},{1... | collective-permute-start | bytes 393224 | tf_op jit(solution)/shard_map/ppermute | solution.py:151
  23.3 2.3 %collective-permute-done.2 = f32[64,512]{1,0:T(8,128)S(1)} collective-permute-done((f32[64,512]{1,0:T(8,128)S(1)}, f32[64,512]{1,0:T(8,128)S(1)}, u32[]{:S(2)}, u32[]{:S(2)}) %collective-permute-start.2) | collective-permute-done | bytes 131104 | tf_op jit(solution)/shard_map/ppermute | solution.py:151
  26.2 5.6 %collective-permute-done.3 = f32[64,512]{1,0:T(8,128)S(1)} collective-permute-done((f32[64,512]{1,0:T(8,128)S(1)}, f32[64,512]{1,0:T(8,128)S(1)}, u32[]{:S(2)}, u32[]{:S(2)}) %collective-permute-start.3) | collective-permute-done | bytes 131104 | tf_op jit(solution)/shard_map/ppermute | solution.py:153
  32.5 3.7 %collective-permute-done.7 = f32[32,512]{1,0:T(8,128)S(1)} collective-permute-done((f32[32,512]{1,0:T(8,128)S(1)}, f32[32,512]{1,0:T(8,128)S(1)}, u32[]{:S(2)}, u32[]{:S(2)}) %collective-permute-start.7) | collective-permute-done | bytes 65568 | tf_op jit(solution)/shard_map/ppermute | solution.py:157
  37.1 7.1 %all-to-all-start = ((bf16[16,32,512]{2,1,0:T(8,128)(2,1)}), bf16[16,32,512]{2,1,0:T(8,128)(2,1)S(1)}, u32[]{:S(2)}, u32[]{:S(2)}) async-start(bf16[16,32,512]{2,1,0:T(8,128)(2,1)} %broadcast_in_dim.5), calls=%async_computation | async-start | bytes 1048576 | tf_op jit(solution)/shard_map/all_to_all | solution.py:24
  44.3 4.3 %copy.8 = bf16[512,1,2304]{0,2,1:T(8,128)(2,1)} copy(bf16[512,1,2304]{2,0,1:T(8,128)(2,1)} %param.5) | data formatting | bytes 4718592 | tf_op args[0]
  49.5 6.0 %all-to-all-done = bf16[16,32,512]{2,1,0:T(8,128)(2,1)S(1)} async-done(((bf16[16,32,512]{2,1,0:T(8,128)(2,1)}), bf16[16,32,512]{2,1,0:T(8,128)(2,1)S(1)}, u32[]{:S(2)}, u32[]{:S(2)}) %all-to-all-start) | async-done | bytes 524320 | tf_op jit(solution)/shard_map/all_to_all | solution.py:24
  55.5 1.9 %copy-done.1 = bf16[512,1,2304]{2,0,1:T(8,128)(2,1)S(1)} copy-done((bf16[512,1,2304]{2,0,1:T(8,128)(2,1)S(1)}, bf16[512,1,2304]{2,0,1:T(8,128)(2,1)}, u32[]{:S(2)}) %copy-start.1) | copy-done | bytes 2359320
  58.2 2.8 %collective-permute-done.8.received_ref = bf16[256,2304]{1,0:T(8,128)(2,1)S(1)} collective-permute-done((bf16[256,2304]{1,0:T(8,128)(2,1)S(1)}, bf16[256,2304]{1,0:T(8,128)(2,1)S(1)}, u32[]{:S(2)}, u32[]{:S(2)}) %collective-permute-start.8) | collective-permute-done | bytes 1179680 | tf_op jit(solution)/shard_map/ppermute | solution.py:167
  61.9 24.7 %all_to_all.25.shares_ref = bf16[8,32,2304]{2,1,0:T(8,128)(2,1)S(1)} all-to-all(bf16[8,32,2304]{2,1,0:T(8,128)(2,1)S(1)} %bitcast.74), channel_id=1, replica_groups={{0,2,4,6,8,10,12,14},{1,3,5,7,9,11,13,15},{16,18,20,22,24,26,28,30},{17..., dimensions={0} | all-to-all | bytes 2359296 | tf_op jit(solution)/shard_map/all_to_all | solution.py:169
  86.8 20.8 %all_to_all.26 = bf16[8,32,2304]{2,1,0:T(8,128)(2,1)S(1)} all-to-all(bf16[8,32,2304]{2,1,0:T(8,128)(2,1)S(1)} %shard_map.78), channel_id=1, replica_groups={{0,2,4,6,8,10,12,14},{1,3,5,7,9,11,13,15},{16,18,20,22,24,26,28,30},{17..., dimensions={0} | all-to-all | bytes 2359296 | tf_op jit(solution)/shard_map/all_to_all | solution.py:182
  108.4 2.0 %collective-permute-done.9.err_ref = bf16[256,2304]{1,0:T(8,128)(2,1)S(1)} collective-permute-done((bf16[256,2304]{1,0:T(8,128)(2,1)S(1)}, bf16[256,2304]{1,0:T(8,128)(2,1)S(1)}, u32[]{:S(2)}, u32[]{:S(2)}) %collective-permute-start.9) | collective-permute-done | bytes 1179680 | tf_op jit(solution)/shard_map/ppermute | solution.py:185
  111.3 20.3 %all_to_all.27 = bf16[16,32,512]{2,1,0:T(8,128)(2,1)S(1)} all-to-all(bf16[16,32,512]{2,1,0:T(8,128)(2,1)S(1)} %bitcast.78), channel_id=1, replica_groups=mesh['layer'=16,'latent'=16] {'layer'}, dimensions={0} | all-to-all | bytes 1048576 | tf_op jit(solution)/shard_map/all_to_all | solution.py:204
  133.2 4.9 %all-to-all-start.4 = ((bf16[16,32,512]{2,1,0:T(8,128)(2,1)}), bf16[16,32,512]{2,1,0:T(8,128)(2,1)}, u32[]{:S(2)}, u32[]{:S(2)}) async-start(bf16[16,32,512]{2,1,0:T(8,128)(2,1)} %broadcast_in_dim.7), calls=%async_computation.4 | async-start | bytes 1048576 | tf_op jit(solution)/shard_map/all_to_all | solution.py:24
  138.1 2.0 %maximum_select_fusion = bf16[512,2304]{1,0:T(8,128)(2,1)S(1)} fusion(bf16[256,2304]{1,0:T(8,128)(2,1)} %copy-done.4, bf16[256,2304]{1,0:T(8,128)(2,1)S(1)} %bitcast.72, pred[]{:T(512)S(6)} %eq.14), kind=kLoop, calls=%fused_computation.2 | loop fusion | flops 10616832 | bytes 4718593 | tf_op jit(solution)/shard_map/jit(_where)/select_n | solution.py:199
  140.1 2.8 %fusion = bf16[512,1,2304]{2,0,1:T(8,128)(2,1)} fusion(bf16[512,512]{1,0:T(8,128)(2,1)S(1)} %bitcast.77, bf16[512,2304]{1,0:T(8,128)(2,1)S(1)} %maximum_select_fusion), kind=kOutput, calls=%fused_computation.1 | convolution fusion | flops 1209139200 | bytes 5242880 | tf_op jit(solution)/shard_map/dot_general | solution.py:210
  142.9 10.5 %all-to-all-done.4 = bf16[16,32,512]{2,1,0:T(8,128)(2,1)} async-done(((bf16[16,32,512]{2,1,0:T(8,128)(2,1)}), bf16[16,32,512]{2,1,0:T(8,128)(2,1)}, u32[]{:S(2)}, u32[]{:S(2)}) %all-to-all-start.4) | async-done | bytes 524320 | tf_op jit(solution)/shard_map/all_to_all | solution.py:24
  153.4 1.7 %copy-done.3 = bf16[512,1,2304]{0,2,1:T(8,128)(2,1)S(1)} copy-done((bf16[512,1,2304]{0,2,1:T(8,128)(2,1)S(1)}, bf16[512,1,2304]{0,2,1:T(8,128)(2,1)}, u32[]{:S(2)}) %copy-start.3) | copy-done | bytes 2359320
  155.1 3.9 %shard_map.81 = bf16[2304,512]{1,0:T(8,128)(2,1)} custom-call(bf16[2304,512]{1,0:T(8,128)(2,1)S(1)} %bitcast.73, bf16[512,512]{1,0:T(8,128)(2,1)} %bitcast.22.grad_ref), custom_call_target="tpu_custom_call" | custom-call | flops 1207959552 | bytes 10616832 | tf_op jit(solution)/shard_map/pallas_call | solution.py:50
  (61 shorter events, 13.9 us)
Async XLA Ops:
  0.6 1.8 %copy-start = (bf16[1,2304,512]{2,1,0:T(8,128)(2,1)S(1)}, bf16[1,2304,512]{2,1,0:T(8,128)(2,1)}, u32[]{:S(2)}) copy-start(bf16[1,2304,512]{2,1,0:T(8,128)(2,1)} %param.6) | copy-start | bytes 7077892
  3.5 9.9 %collective-permute-start.4 = (f32[64,512]{1,0:T(8,128)S(1)}, f32[64,512]{1,0:T(8,128)S(1)}, u32[]{:S(2)}, u32[]{:S(2)}) collective-permute-start(f32[64,512]{1,0:T(8,128)S(1)} %fusion.13), channel_id=1, source_target_pairs={{16,0},{32,16},{48,32},{64,48},{80,64},{96,80},{112,96},{0,112},{1... | collective-permute-start | bytes 393224 | tf_op jit(solution)/shard_map/ppermute | solution.py:147
  3.7 9.1 %collective-permute-start = (f32[64,512]{1,0:T(8,128)S(1)}, f32[64,512]{1,0:T(8,128)S(1)}, u32[]{:S(2)}, u32[]{:S(2)}) collective-permute-start(f32[64,512]{1,0:T(8,128)S(1)} %fusion.15), channel_id=1, source_target_pairs={{0,16},{16,32},{32,48},{48,64},{64,80},{80,96},{96,112},{112,0},{1... | collective-permute-start | bytes 393224 | tf_op jit(solution)/shard_map/ppermute | solution.py:147
  13.3 6.0 %collective-permute-start.1 = (f32[64,512]{1,0:T(8,128)S(1)}, f32[64,512]{1,0:T(8,128)S(1)}, u32[]{:S(2)}, u32[]{:S(2)}) collective-permute-start(f32[64,512]{1,0:T(8,128)S(1)} %fusion.17), channel_id=1, source_target_pairs={{0,16},{16,32},{32,48},{48,64},{64,80},{80,96},{96,112},{112,0},{1... | collective-permute-start | bytes 393224 | tf_op jit(solution)/shard_map/ppermute | solution.py:149
  13.9 6.0 %collective-permute-start.5 = (f32[64,512]{1,0:T(8,128)S(1)}, f32[64,512]{1,0:T(8,128)S(1)}, u32[]{:S(2)}, u32[]{:S(2)}) collective-permute-start(f32[64,512]{1,0:T(8,128)S(1)} %fusion.20), channel_id=1, source_target_pairs={{16,0},{32,16},{48,32},{64,48},{80,64},{96,80},{112,96},{0,112},{1... | collective-permute-start | bytes 393224 | tf_op jit(solution)/shard_map/ppermute | solution.py:149
  19.3 6.3 %collective-permute-start.2 = (f32[64,512]{1,0:T(8,128)S(1)}, f32[64,512]{1,0:T(8,128)S(1)}, u32[]{:S(2)}, u32[]{:S(2)}) collective-permute-start(f32[64,512]{1,0:T(8,128)S(1)} %add.139), channel_id=1, source_target_pairs={{0,16},{16,32},{32,48},{48,64},{64,80},{80,96},{96,112},{112,0},{1... | collective-permute-start | bytes 393224 | tf_op jit(solution)/shard_map/ppermute | solution.py:151
  19.9 16.3 %copy-start.13 = (f32[512]{0:T(512)S(1)}, f32[512]{0:T(512)}, u32[]{:S(2)}) copy-start(f32[512]{0:T(512)} %param.8) | copy-start | bytes 6148
  20.0 6.3 %collective-permute-start.6 = (f32[64,512]{1,0:T(8,128)S(1)}, f32[64,512]{1,0:T(8,128)S(1)}, u32[]{:S(2)}, u32[]{:S(2)}) collective-permute-start(f32[64,512]{1,0:T(8,128)S(1)} %add.151), channel_id=1, source_target_pairs={{16,0},{32,16},{48,32},{64,48},{80,64},{96,80},{112,96},{0,112},{1... | collective-permute-start | bytes 393224 | tf_op jit(solution)/shard_map/ppermute | solution.py:151
  25.6 6.3 %collective-permute-start.3 = (f32[64,512]{1,0:T(8,128)S(1)}, f32[64,512]{1,0:T(8,128)S(1)}, u32[]{:S(2)}, u32[]{:S(2)}) collective-permute-start(f32[64,512]{1,0:T(8,128)S(1)} %add.143), channel_id=1, source_target_pairs={{0,16},{16,32},{32,48},{48,64},{64,80},{80,96},{96,112},{112,0},{1... | collective-permute-start | bytes 393224 | tf_op jit(solution)/shard_map/ppermute | solution.py:153
  31.9 5.3 %copy-start.8 = (f32[64,512]{1,0:T(8,128)}, f32[64,512]{1,0:T(8,128)S(1)}, u32[]{:S(2)}) copy-start(f32[64,512]{1,0:T(8,128)S(1)} %add_add_fusion) | copy-start | bytes 393220
  31.9 4.4 %collective-permute-start.7 = (f32[32,512]{1,0:T(8,128)S(1)}, f32[32,512]{1,0:T(8,128)S(1)}, u32[]{:S(2)}, u32[]{:S(2)}) collective-permute-start(f32[32,512]{1,0:T(8,128)S(1)} %dynamic-slice_bitcast_fusion.1), channel_id=1, source_target_pairs={{0,128},{16,144},{32,160},{48,176},{64,192},{80,208},{96,224},{112... | collective-permute-start | bytes 196616 | tf_op jit(solution)/shard_map/ppermute | solution.py:157
  37.1 18.3 %all-to-all-start = ((bf16[16,32,512]{2,1,0:T(8,128)(2,1)}), bf16[16,32,512]{2,1,0:T(8,128)(2,1)S(1)}, u32[]{:S(2)}, u32[]{:S(2)}) async-start(bf16[16,32,512]{2,1,0:T(8,128)(2,1)} %broadcast_in_dim.5), calls=%async_computation | async-start | bytes 1048576 | tf_op jit(solution)/shard_map/all_to_all | solution.py:24
  55.5 6.4 %copy-start.5 = (bf16[16,32,512]{2,1,0:T(8,128)(2,1)}, bf16[16,32,512]{2,1,0:T(8,128)(2,1)S(1)}, u32[]{:S(2)}) copy-start(bf16[16,32,512]{2,1,0:T(8,128)(2,1)S(1)} %all-to-all-done) | copy-start | bytes 1572868
  55.5 1.9 %copy-start.1 = (bf16[512,1,2304]{2,0,1:T(8,128)(2,1)S(1)}, bf16[512,1,2304]{2,0,1:T(8,128)(2,1)}, u32[]{:S(2)}) copy-start(bf16[512,1,2304]{2,0,1:T(8,128)(2,1)} %param.7) | copy-start | bytes 7077892
  58.1 2.9 %collective-permute-start.8 = (bf16[256,2304]{1,0:T(8,128)(2,1)S(1)}, bf16[256,2304]{1,0:T(8,128)(2,1)S(1)}, u32[]{:S(2)}, u32[]{:S(2)}) collective-permute-start(bf16[256,2304]{1,0:T(8,128)(2,1)S(1)} %shard_map.76), channel_id=1, source_target_pairs={{0,1},{1,0},{2,3},{3,2},{4,5},{5,4},{6,7},{7,6},{8,9},{9,8},{10,11... | collective-permute-start | bytes 3538952 | tf_op jit(solution)/shard_map/ppermute | solution.py:167
  61.9 24.7 %copy-start.7 = (f32[1,2304]{1,0:T(1,128)S(1)}, f32[1,2304]{1,0:T(1,128)}, u32[]{:S(2)}) copy-start(f32[1,2304]{1,0:T(1,128)} %bias_ref.1) | copy-start | bytes 27652
  86.6 21.0 %copy-start.2 = (bf16[512,1,2304]{2,0,1:T(8,128)(2,1)S(1)}, bf16[512,1,2304]{2,0,1:T(8,128)(2,1)}, u32[]{:S(2)}) copy-start(bf16[512,1,2304]{2,0,1:T(8,128)(2,1)} %param.7) | copy-start | bytes 7077892
  107.6 2.8 %collective-permute-start.9 = (bf16[256,2304]{1,0:T(8,128)(2,1)S(1)}, bf16[256,2304]{1,0:T(8,128)(2,1)S(1)}, u32[]{:S(2)}, u32[]{:S(2)}) collective-permute-start(bf16[256,2304]{1,0:T(8,128)(2,1)S(1)} %bitcast.70), channel_id=1, source_target_pairs={{0,1},{1,0},{2,3},{3,2},{4,5},{5,4},{6,7},{7,6},{8,9},{9,8},{10,11... | collective-permute-start | bytes 3538952 | tf_op jit(solution)/shard_map/ppermute | solution.py:185
  108.4 23.2 %copy-start.9 = (f32[64,512]{1,0:T(8,128)S(1)}, f32[64,512]{1,0:T(8,128)}, u32[]{:S(2)}) copy-start(f32[64,512]{1,0:T(8,128)} %copy-done.8) | copy-start | bytes 393220
  108.4 23.2 %copy-start.12 = (f32[32,512]{1,0:T(8,128)S(1)}, f32[32,512]{1,0:T(8,128)}, u32[]{:S(2)}) copy-start(f32[32,512]{1,0:T(8,128)} %copy-done.11) | copy-start | bytes 196612
  110.4 21.1 %copy-start.4 = (bf16[256,2304]{1,0:T(8,128)(2,1)}, bf16[256,2304]{1,0:T(8,128)(2,1)S(1)}, u32[]{:S(2)}) copy-start(bf16[256,2304]{1,0:T(8,128)(2,1)S(1)} %collective-permute-done.9.err_ref) | copy-start | bytes 3538948
  133.2 20.3 %all-to-all-start.4 = ((bf16[16,32,512]{2,1,0:T(8,128)(2,1)}), bf16[16,32,512]{2,1,0:T(8,128)(2,1)}, u32[]{:S(2)}, u32[]{:S(2)}) async-start(bf16[16,32,512]{2,1,0:T(8,128)(2,1)} %broadcast_in_dim.7), calls=%async_computation.4 | async-start | bytes 1048576 | tf_op jit(solution)/shard_map/all_to_all | solution.py:24
  138.1 2.0 %copy-start.6 = (bf16[16,32,512]{2,1,0:T(8,128)(2,1)S(1)}, bf16[16,32,512]{2,1,0:T(8,128)(2,1)}, u32[]{:S(2)}) copy-start(bf16[16,32,512]{2,1,0:T(8,128)(2,1)} %copy-done.5) | copy-start | bytes 1572868
  153.4 1.7 %copy-start.3 = (bf16[512,1,2304]{0,2,1:T(8,128)(2,1)S(1)}, bf16[512,1,2304]{0,2,1:T(8,128)(2,1)}, u32[]{:S(2)}) copy-start(bf16[512,1,2304]{0,2,1:T(8,128)(2,1)} %copy.8) | copy-start | bytes 7077892
  (2 other events, 1.5 us)

commit v4 on v3

--- a/solution.py
+++ b/solution.py
@@ -16,6 +16,7 @@
 
 Z_UP = [(x * 8 + z, x * 8 + (z + 1) % 8) for x in range(2) for z in range(8)]
 Z_DOWN = [(b, a) for a, b in Z_UP]
+Z_ACROSS = [(a, b ^ 8) for a, b in Z_UP]
 X_NEXT = [(i, (i + 8) % 16) for i in range(16)]
 
 
@@ -25,7 +26,6 @@
 
 
 SMALL = pl.BlockSpec(memory_space=pltpu.SMEM)
-LARGE = pl.BlockSpec(memory_space=pl.ANY)
 STORED = pl.BlockSpec(memory_space=pltpu.HBM)
 NT = (((1,), (1,)), ((), ()))
 PIECES = 3
@@ -46,7 +46,7 @@
     return call(kernel, out_shape, whole(out_shape), specs, [], flops, moved, *operands)
 
 
-def call(kernel, out_shape, out_spec, specs, scratch, flops, moved, *operands):
+def call(kernel, out_shape, out_spec, specs, scratch, flops, moved, *operands, room=20):
     return pl.pallas_call(
         kernel,
         out_shape=out_shape,
@@ -54,7 +54,7 @@
         in_specs=specs,
         out_specs=out_spec,
         scratch_shapes=scratch,
-        compiler_params=pltpu.CompilerParams(vmem_limit_bytes=20 * 1024 * 1024),
+        compiler_params=pltpu.CompilerParams(vmem_limit_bytes=room * 1024 * 1024),
         cost_estimate=pl.CostEstimate(flops=flops, bytes_accessed=moved, transcendentals=0),
     )(*operands)
 
@@ -99,24 +99,10 @@
     out_ref[pl.ds(pl.multiple_of((1 - core) * half, half), half), :] = other.astype(BF16)
 
 
-def enc_kernel(acts_ref, grad_ref, out_ref, acts_buf, out_buf, sems):
-    step = acts_ref.shape[0] // PIECES
-    rows = [slice(i * step, (i + 1) * step) for i in range(PIECES)]
-    loads = [
-        pltpu.make_async_copy(acts_ref.at[r], acts_buf.at[r], sems.at[0, i])
-        for i, r in enumerate(rows)
-    ]
-    for load in loads:
-        load.start()
-    grad = grad_ref[...]
-    stores = []
-    for i, r in enumerate(rows):
-        loads[i].wait()
-        out_buf[r] = jnp.dot(acts_buf[r], grad, preferred_element_type=F32).astype(BF16)
-        stores.append(pltpu.make_async_copy(out_buf.at[r], out_ref.at[r], sems.at[1, i]))
-        stores[-1].start()
-    for store in stores:
-        store.wait()
+def enc_kernel(acts_ref, grad_ref, out_ref):
+    out_ref[...] = jnp.dot(
+        acts_ref[...], grad_ref[...], preferred_element_type=F32
+    ).astype(BF16)
 
 
 def local(acts, enc_weight, dec_weight, enc_bias, dec_bias):
@@ -149,12 +135,18 @@
     up, down = lax.ppermute(up, "layer", Z_UP), lax.ppermute(down, "layer", Z_DOWN)
     up, down = up + partial(2), down + partial(-1)
     up, down = lax.ppermute(up, "layer", Z_UP), lax.ppermute(down, "layer", Z_DOWN)
-    own = partial(0)
-    up = lax.ppermute(up + partial(1), "layer", Z_UP)
-    column = (up + (down + own)).reshape(2, rows, local_latents)
-    kept_column = lax.dynamic_index_in_dim(column, x_lo, 0, keepdims=False)
-    sent_column = lax.dynamic_index_in_dim(column, 1 - x_lo, 0, keepdims=False)
-    own_pre = kept_column + lax.ppermute(sent_column, "layer", X_NEXT) + enc_bias[None, :]
+    up = (up + partial(1)).reshape(2, rows, local_latents)
+    down = (down + partial(0)).reshape(2, rows, local_latents)
+
+    def column(x, at):
+        return lax.dynamic_index_in_dim(x, at, 0, keepdims=False)
+
+    arrived = (
+        lax.ppermute(column(up, 1 - x_lo), "layer", Z_ACROSS),
+        lax.ppermute(column(up, x_lo), "layer", Z_UP),
+        lax.ppermute(column(down, 1 - x_lo), "layer", X_NEXT),
+    )
+    own_pre = column(down, x_lo) + sum(arrived) + enc_bias[None, :]
     own_latents = jnp.maximum(own_pre, 0.0).astype(BF16)
     latents = spread(own_latents, "layer").reshape(tokens, local_latents)
 
@@ -206,26 +198,22 @@
     )
     latent_grad = jnp.sum(back_parts.astype(F32), axis=0)
     own_grad_pre = jnp.where(own_pre > 0, latent_grad, 0.0).astype(BF16)
-    latents_late, err_late, latent_grad = lax.optimization_barrier((latents, err, latent_grad))
     dec_grad = lax.dot_general(
-        latents_late, err_late, (((0,), (0,)), ((), ())), preferred_element_type=F32
+        latents, err, (((0,), (0,)), ((), ())), preferred_element_type=F32
     ).astype(BF16)
+    own_grad_pre, dec_grad = lax.optimization_barrier((own_grad_pre, dec_grad))
     grad_pre = spread(own_grad_pre, "layer").reshape(tokens, local_latents)
-    enc_grad = call(
+    enc_grad = pl.pallas_call(
         enc_kernel,
-        shape((width, local_latents), BF16),
-        STORED,
-        [LARGE, whole(grad_pre)],
-        [
-            pltpu.VMEM((width, tokens), BF16),
-            pltpu.VMEM((width, local_latents), BF16),
-            pltpu.SemaphoreType.DMA((2, PIECES)),
-        ],
-        2 * tokens * width * local_latents,
-        3 * moved,
-        acts_t,
-        grad_pre,
-    )
+        out_shape=shape((width, local_latents), BF16),
+        grid=(2,),
+        in_specs=[pl.BlockSpec((width // 2, tokens), lambda i: (i, 0)), whole(grad_pre)],
+        out_specs=pl.BlockSpec((width // 2, local_latents), lambda i: (i, 0)),
+        compiler_params=pltpu.CompilerParams(vmem_limit_bytes=16 * 1024 * 1024),
+        cost_estimate=pl.CostEstimate(
+            flops=2 * tokens * width * local_latents, bytes_accessed=3 * moved, transcendentals=0
+        ),
+    )(acts_t, grad_pre)
     return (
         latent_grad,
         enc_grad.reshape(layers_here, width, local_latents),

time: 160 us -> 156 us (0.975)
  waiting for transfers between devices: 39.9 us -> 30.6 us
  starting transfers between devices: 21.4 us -> 27.5 us
  local copies, waits for them, and re-layouts: 14.4 us -> 12.4 us
  matrix products: 6.97 us -> 8.81 us
    all_to_all x0 -> x1, waiting for transfers between devices: none -> 11.4 us  [local(): lax.all_to_all(back.reshape(16, rows, local_latents), 'layer', 0, 0)]
    all_to_all x2 -> x1, waiting for transfers between devices: 16.5 us -> 6.28 us  [spread(): return lax.all_to_all(copies, axis, 0, 0, axis_index_groups=groups)]
    ppermute x2 -> x3, waiting for transfers between devices: 9.35 us -> 2.77 us  [the longest x1 1.71 us: local(): lax.ppermute(column(down, 1 - x_lo), 'layer', X_NEXT)]
    all_to_all x0 -> x1, starting transfers between devices: none -> 4.83 us  [local(): lax.all_to_all(back.reshape(16, rows, local_latents), 'layer', 0, 0)]
    ppermute x3, waiting for transfers between devices: 9.16 us -> 4.62 us  [local(): lax.ppermute(up, 'layer', Z_UP)]
    ppermute x2 -> x3, starting transfers between devices: 0.7 us -> 5.14 us  [the longest x1 3.47 us: local(): lax.ppermute(column(up, x_lo), 'layer', Z_UP)]
    pallas_call x6 -> x5, Pallas kernels: 7.25 us -> 3.37 us  [call(): pl.pallas_call(kernel, out_shape=out_shape, grid=(1,), in_specs=specs, ou...]
    all_to_all x2 -> x1, starting transfers between devices: 12 us -> 8.21 us  [spread(): return lax.all_to_all(copies, axis, 0, 0, axis_index_groups=groups)]
  transfers between devices with their start and end apart: 12 -> 13, of which waited for: 9 -> 11; matrix products, arithmetic and copies ran while one was open for 9% -> 9% of each run, Pallas kernels for 1% -> 1%
where the time goes in v4:
time: 156 us; the launch traced here: 155 us
  blocking collectives  65.8 us (42%)
  waiting for transfers between devices  30.6 us (20%)
  starting transfers between devices  27.5 us (18%)
  local copies, waits for them, and re-layouts  12.4 us (8%)
  matrix products  8.81 us (6%)
  Pallas kernels  5.95 us (4%)
  other arithmetic  2.86 us (2%)
    all_to_all x1, blocking collectives, local(): lax.all_to_all(chip_sum.reshape(8, rows, width), 'latent', 0, 0, axis_ind...  24.8 us
    all_to_all x1, blocking collectives, local(): lax.all_to_all(err_copies, 'latent', 0, 0, axis_index_groups=CHIP_GROUPS)  20.8 us
    all_to_all x1, blocking collectives, spread(): return lax.all_to_all(copies, axis, 0, 0, axis_index_groups=groups)  20.2 us
    all_to_all x1, waiting for transfers between devices, local(): lax.all_to_all(back.reshape(16, rows, local_latents), 'layer', 0, 0)  11.4 us
    all_to_all x1, starting transfers between devices, spread(): return lax.all_to_all(copies, axis, 0, 0, axis_index_groups=groups)  8.21 us
    unnamed x21, local copies, waits for them, and re-layouts  7.72 us
    all_to_all x1, waiting for transfers between devices, spread(): return lax.all_to_all(copies, axis, 0, 0, axis_index_groups=groups)  6.28 us
    ppermute x3, starting transfers between devices, local(): lax.ppermute(down, 'layer', Z_DOWN)  5.15 us
  transfers between devices with their start and end apart: 13, of which 11 were waited for; matrix products, arithmetic and copies ran while one was open for 9% of the time, Pallas kernels for 1%

profile of v4, /device:TPU:34, one launch (start us, length us, event | category | flops | bytes accessed | tf_op | source)
XLA Modules:
  0.0 154.8 jit_solution(13023028729882610458)
XLA Ops:
  3.5 2.0 %collective-permute-start.3 = (f32[64,512]{1,0:T(8,128)S(1)}, f32[64,512]{1,0:T(8,128)S(1)}, u32[]{:S(2)}, u32[]{:S(2)}) collective-permute-start(f32[64,512]{1,0:T(8,128)S(1)} %fusion.19), channel_id=1, source_target_pairs={{0,16},{16,32},{32,48},{48,64},{64,80},{80,96},{96,112},{112,0},{1... | collective-permute-start | bytes 393224 | tf_op jit(solution)/shard_map/ppermute | solution.py:133
  5.6 1.6 %constant_dynamic-slice_fusion = (bf16[2,1,32,2304]{3,2,1,0:T(8,128)(2,1)S(1)}, bf16[2,1,32,2304]{3,2,1,0:T(8,128)(2,1)S(1)}, bf16[2,1,32,2304]{3,2,1,0:T(8,128)...) fusion(bf16[2,8,32,2304]{3,2,1,0:T(8,128)(2,1)} %bitcast.81, ...), kind=kLoop, calls=%fused_computation.35 | loop fusion | bytes 3538968 | tf_op jit(solution)/shard_map/jit(dynamic_index_in_dim)/dynamic_slice | solution.py:128
  9.4 2.0 %collective-permute-start.4 = (f32[64,512]{1,0:T(8,128)S(1)}, f32[64,512]{1,0:T(8,128)S(1)}, u32[]{:S(2)}, u32[]{:S(2)}) collective-permute-start(f32[64,512]{1,0:T(8,128)S(1)} %fusion.25), channel_id=1, source_target_pairs={{0,16},{16,32},{32,48},{48,64},{64,80},{80,96},{96,112},{112,0},{1... | collective-permute-start | bytes 393224 | tf_op jit(solution)/shard_map/ppermute | solution.py:135
  11.9 2.4 %collective-permute-start.1 = (f32[64,512]{1,0:T(8,128)S(1)}, f32[64,512]{1,0:T(8,128)S(1)}, u32[]{:S(2)}, u32[]{:S(2)}) collective-permute-start(f32[64,512]{1,0:T(8,128)S(1)} %fusion.22), channel_id=1, source_target_pairs={{16,0},{32,16},{48,32},{64,48},{80,64},{96,80},{112,96},{0,112},{1... | collective-permute-start | bytes 393224 | tf_op jit(solution)/shard_map/ppermute | solution.py:135
  14.8 1.8 %collective-permute-done.4 = f32[64,512]{1,0:T(8,128)S(1)} collective-permute-done((f32[64,512]{1,0:T(8,128)S(1)}, f32[64,512]{1,0:T(8,128)S(1)}, u32[]{:S(2)}, u32[]{:S(2)}) %collective-permute-start.4) | collective-permute-done | bytes 131104 | tf_op jit(solution)/shard_map/ppermute | solution.py:135
  17.5 2.6 %collective-permute-start.2 = (f32[64,512]{1,0:T(8,128)S(1)}, f32[64,512]{1,0:T(8,128)S(1)}, u32[]{:S(2)}, u32[]{:S(2)}) collective-permute-start(f32[64,512]{1,0:T(8,128)S(1)} %add.145), channel_id=1, source_target_pairs={{16,0},{32,16},{48,32},{64,48},{80,64},{96,80},{112,96},{0,112},{1... | collective-permute-start | bytes 393224 | tf_op jit(solution)/shard_map/ppermute | solution.py:137
  20.7 2.2 %collective-permute-done.5 = f32[64,512]{1,0:T(8,128)S(1)} collective-permute-done((f32[64,512]{1,0:T(8,128)S(1)}, f32[64,512]{1,0:T(8,128)S(1)}, u32[]{:S(2)}, u32[]{:S(2)}) %collective-permute-start.5) | collective-permute-done | bytes 131104 | tf_op jit(solution)/shard_map/ppermute | solution.py:137
  23.0 3.5 %collective-permute-start.7 = (f32[32,512]{1,0:T(8,128)S(1)}, f32[32,512]{1,0:T(8,128)S(1)}, u32[]{:S(2)}, u32[]{:S(2)}) collective-permute-start(f32[32,512]{1,0:T(8,128)S(1)} %get-tuple-element.29), channel_id=1, source_target_pairs={{0,16},{16,32},{32,48},{48,64},{64,80},{80,96},{96,112},{112,0},{1... | collective-permute-start | bytes 196616 | tf_op jit(solution)/shard_map/ppermute | solution.py:146
  26.6 1.6 %collective-permute-start.8 = (f32[32,512]{1,0:T(8,128)S(1)}, f32[32,512]{1,0:T(8,128)S(1)}, u32[]{:S(2)}, u32[]{:S(2)}) collective-permute-start(f32[32,512]{1,0:T(8,128)S(1)} %dynamic-slice_bitcast_fusion.1), channel_id=1, source_target_pairs={{0,128},{16,144},{32,160},{48,176},{64,192},{80,208},{96,224},{112... | collective-permute-start | bytes 196616 | tf_op jit(solution)/shard_map/ppermute | solution.py:147
  29.2 1.7 %collective-permute-done.8 = f32[32,512]{1,0:T(8,128)S(1)} collective-permute-done((f32[32,512]{1,0:T(8,128)S(1)}, f32[32,512]{1,0:T(8,128)S(1)}, u32[]{:S(2)}, u32[]{:S(2)}) %collective-permute-start.8) | collective-permute-done | bytes 65568 | tf_op jit(solution)/shard_map/ppermute | solution.py:147
  32.4 8.2 %all-to-all-start = ((bf16[16,32,512]{2,1,0:T(8,128)(2,1)}), bf16[16,32,512]{2,1,0:T(8,128)(2,1)S(1)}, u32[]{:S(2)}, u32[]{:S(2)}) async-start(bf16[16,32,512]{2,1,0:T(8,128)(2,1)} %broadcast_in_dim.5), calls=%async_computation | async-start | bytes 1048576 | tf_op jit(solution)/shard_map/all_to_all | solution.py:25
  40.6 4.3 %copy.8 = bf16[512,1,2304]{0,2,1:T(8,128)(2,1)} copy(bf16[512,1,2304]{2,0,1:T(8,128)(2,1)} %param.5) | data formatting | bytes 4718592 | tf_op args[0]
  45.8 6.3 %all-to-all-done = bf16[16,32,512]{2,1,0:T(8,128)(2,1)S(1)} async-done(((bf16[16,32,512]{2,1,0:T(8,128)(2,1)}), bf16[16,32,512]{2,1,0:T(8,128)(2,1)S(1)}, u32[]{:S(2)}, u32[]{:S(2)}) %all-to-all-start) | async-done | bytes 524320 | tf_op jit(solution)/shard_map/all_to_all | solution.py:25
  52.1 1.9 %copy-done.1 = bf16[512,1,2304]{2,0,1:T(8,128)(2,1)S(1)} copy-done((bf16[512,1,2304]{2,0,1:T(8,128)(2,1)S(1)}, bf16[512,1,2304]{2,0,1:T(8,128)(2,1)}, u32[]{:S(2)}) %copy-start.1) | copy-done | bytes 2359320
  54.8 2.8 %collective-permute-done.9.received_ref = bf16[256,2304]{1,0:T(8,128)(2,1)S(1)} collective-permute-done((bf16[256,2304]{1,0:T(8,128)(2,1)S(1)}, bf16[256,2304]{1,0:T(8,128)(2,1)S(1)}, u32[]{:S(2)}, u32[]{:S(2)}) %collective-permute-start.9) | collective-permute-done | bytes 1179680 | tf_op jit(solution)/shard_map/ppermute | solution.py:159
  58.5 24.8 %all_to_all.25.shares_ref = bf16[8,32,2304]{2,1,0:T(8,128)(2,1)S(1)} all-to-all(bf16[8,32,2304]{2,1,0:T(8,128)(2,1)S(1)} %bitcast.74), channel_id=1, replica_groups={{0,2,4,6,8,10,12,14},{1,3,5,7,9,11,13,15},{16,18,20,22,24,26,28,30},{17..., dimensions={0} | all-to-all | bytes 2359296 | tf_op jit(solution)/shard_map/all_to_all | solution.py:161
  83.5 20.8 %all_to_all.26 = bf16[8,32,2304]{2,1,0:T(8,128)(2,1)S(1)} all-to-all(bf16[8,32,2304]{2,1,0:T(8,128)(2,1)S(1)} %shard_map.78), channel_id=1, replica_groups={{0,2,4,6,8,10,12,14},{1,3,5,7,9,11,13,15},{16,18,20,22,24,26,28,30},{17..., dimensions={0} | all-to-all | bytes 2359296 | tf_op jit(solution)/shard_map/all_to_all | solution.py:174
  105.1 2.0 %collective-permute-done.10.err_ref = bf16[256,2304]{1,0:T(8,128)(2,1)S(1)} collective-permute-done((bf16[256,2304]{1,0:T(8,128)(2,1)S(1)}, bf16[256,2304]{1,0:T(8,128)(2,1)S(1)}, u32[]{:S(2)}, u32[]{:S(2)}) %collective-permute-start.10) | collective-permute-done | bytes 1179680 | tf_op jit(solution)/shard_map/ppermute | solution.py:177
  108.9 4.8 %all-to-all-start.3 = ((bf16[16,32,512]{2,1,0:T(8,128)(2,1)}), bf16[16,32,512]{2,1,0:T(8,128)(2,1)}, u32[]{:S(2)}, u32[]{:S(2)}) async-start(bf16[16,32,512]{2,1,0:T(8,128)(2,1)} %bitcast.78), calls=%async_computation.3 | async-start | bytes 1048576 | tf_op jit(solution)/shard_map/all_to_all | solution.py:196
  113.8 4.7 %convolution_convert_fusion = bf16[512,2304]{1,0:T(8,128)(2,1)} fusion(bf16[512,512]{1,0:T(8,128)(2,1)} %bitcast.77, bf16[256,2304]{1,0:T(8,128)(2,1)} %copy-done.6, bf16[256,2304]{1,0:T(8,128)(2,1)S(1)} %bitcast.73, pred[]{:T(512)S(6)} %eq.14), kind=kOutput, calls=%fused_computation | convolution fusion | flops 1219756032 | bytes 5242881 | tf_op jit(solution)/shard_map/dot_general | solution.py:201
  118.5 11.4 %all-to-all-done.3 = bf16[16,32,512]{2,1,0:T(8,128)(2,1)} async-done(((bf16[16,32,512]{2,1,0:T(8,128)(2,1)}), bf16[16,32,512]{2,1,0:T(8,128)(2,1)}, u32[]{:S(2)}, u32[]{:S(2)}) %all-to-all-start.3) | async-done | bytes 524320 | tf_op jit(solution)/shard_map/all_to_all | solution.py:196
  129.8 1.3 convert_reduce_fusion
  132.0 20.2 %all_to_all.27 = bf16[16,32,512]{2,1,0:T(8,128)(2,1)S(1)} all-to-all(bf16[16,32,512]{2,1,0:T(8,128)(2,1)S(1)} %broadcast_in_dim.7), channel_id=1, replica_groups=mesh['layer'=16,'latent'=16] {'layer'}, dimensions={0} | all-to-all | bytes 1048576 | tf_op jit(solution)/shard_map/all_to_all | solution.py:25
  152.3 2.6 %shard_map.81 = bf16[2304,512]{1,0:T(8,128)(2,1)} custom-call(bf16[2304,512]{1,0:T(8,128)(2,1)S(1)} %bitcast.70, bf16[512,512]{1,0:T(8,128)(2,1)S(1)} %bitcast.79), custom_call_target="tpu_custom_call" | custom-call | flops 1207959552 | bytes 10616832 | tf_op jit(solution)/shard_map/pallas_call | solution.py:206
  (55 shorter events, 16.6 us)
Async XLA Ops:
  0.6 1.8 %copy-start = (bf16[1,2304,512]{2,1,0:T(8,128)(2,1)S(1)}, bf16[1,2304,512]{2,1,0:T(8,128)(2,1)}, u32[]{:S(2)}) copy-start(bf16[1,2304,512]{2,1,0:T(8,128)(2,1)} %param.6) | copy-start | bytes 7077892
  3.5 5.3 %collective-permute-start.3 = (f32[64,512]{1,0:T(8,128)S(1)}, f32[64,512]{1,0:T(8,128)S(1)}, u32[]{:S(2)}, u32[]{:S(2)}) collective-permute-start(f32[64,512]{1,0:T(8,128)S(1)} %fusion.19), channel_id=1, source_target_pairs={{0,16},{16,32},{32,48},{48,64},{64,80},{80,96},{96,112},{112,0},{1... | collective-permute-start | bytes 393224 | tf_op jit(solution)/shard_map/ppermute | solution.py:133
  5.5 5.8 %collective-permute-start = (f32[64,512]{1,0:T(8,128)S(1)}, f32[64,512]{1,0:T(8,128)S(1)}, u32[]{:S(2)}, u32[]{:S(2)}) collective-permute-start(f32[64,512]{1,0:T(8,128)S(1)} %fusion.17), channel_id=1, source_target_pairs={{16,0},{32,16},{48,32},{64,48},{80,64},{96,80},{112,96},{0,112},{1... | collective-permute-start | bytes 393224 | tf_op jit(solution)/shard_map/ppermute | solution.py:133
  9.4 7.3 %collective-permute-start.4 = (f32[64,512]{1,0:T(8,128)S(1)}, f32[64,512]{1,0:T(8,128)S(1)}, u32[]{:S(2)}, u32[]{:S(2)}) collective-permute-start(f32[64,512]{1,0:T(8,128)S(1)} %fusion.25), channel_id=1, source_target_pairs={{0,16},{16,32},{32,48},{48,64},{64,80},{80,96},{96,112},{112,0},{1... | collective-permute-start | bytes 393224 | tf_op jit(solution)/shard_map/ppermute | solution.py:135
  11.9 5.6 %collective-permute-start.1 = (f32[64,512]{1,0:T(8,128)S(1)}, f32[64,512]{1,0:T(8,128)S(1)}, u32[]{:S(2)}, u32[]{:S(2)}) collective-permute-start(f32[64,512]{1,0:T(8,128)S(1)} %fusion.22), channel_id=1, source_target_pairs={{16,0},{32,16},{48,32},{64,48},{80,64},{96,80},{112,96},{0,112},{1... | collective-permute-start | bytes 393224 | tf_op jit(solution)/shard_map/ppermute | solution.py:135
  14.8 16.1 %copy-start.9 = (f32[512]{0:T(512)S(1)}, f32[512]{0:T(512)}, u32[]{:S(2)}) copy-start(f32[512]{0:T(512)} %param.8) | copy-start | bytes 6148
  16.6 6.3 %collective-permute-start.5 = (f32[64,512]{1,0:T(8,128)S(1)}, f32[64,512]{1,0:T(8,128)S(1)}, u32[]{:S(2)}, u32[]{:S(2)}) collective-permute-start(f32[64,512]{1,0:T(8,128)S(1)} %add.157), channel_id=1, source_target_pairs={{0,16},{16,32},{32,48},{48,64},{64,80},{80,96},{96,112},{112,0},{1... | collective-permute-start | bytes 393224 | tf_op jit(solution)/shard_map/ppermute | solution.py:137
  17.5 9.0 %collective-permute-start.2 = (f32[64,512]{1,0:T(8,128)S(1)}, f32[64,512]{1,0:T(8,128)S(1)}, u32[]{:S(2)}, u32[]{:S(2)}) collective-permute-start(f32[64,512]{1,0:T(8,128)S(1)} %add.145), channel_id=1, source_target_pairs={{16,0},{32,16},{48,32},{64,48},{80,64},{96,80},{112,96},{0,112},{1... | collective-permute-start | bytes 393224 | tf_op jit(solution)/shard_map/ppermute | solution.py:137
  22.9 5.5 %collective-permute-start.6 = (f32[32,512]{1,0:T(8,128)S(1)}, f32[32,512]{1,0:T(8,128)S(1)}, u32[]{:S(2)}, u32[]{:S(2)}) collective-permute-start(f32[32,512]{1,0:T(8,128)S(1)} %get-tuple-element.30), channel_id=1, source_target_pairs={{0,144},{16,160},{32,176},{48,192},{64,208},{80,224},{96,240},{112... | collective-permute-start | bytes 196616 | tf_op jit(solution)/shard_map/ppermute | solution.py:145
  23.0 6.2 %collective-permute-start.7 = (f32[32,512]{1,0:T(8,128)S(1)}, f32[32,512]{1,0:T(8,128)S(1)}, u32[]{:S(2)}, u32[]{:S(2)}) collective-permute-start(f32[32,512]{1,0:T(8,128)S(1)} %get-tuple-element.29), channel_id=1, source_target_pairs={{0,16},{16,32},{32,48},{48,64},{64,80},{80,96},{96,112},{112,0},{1... | collective-permute-start | bytes 196616 | tf_op jit(solution)/shard_map/ppermute | solution.py:146
  26.6 4.4 %collective-permute-start.8 = (f32[32,512]{1,0:T(8,128)S(1)}, f32[32,512]{1,0:T(8,128)S(1)}, u32[]{:S(2)}, u32[]{:S(2)}) collective-permute-start(f32[32,512]{1,0:T(8,128)S(1)} %dynamic-slice_bitcast_fusion.1), channel_id=1, source_target_pairs={{0,128},{16,144},{32,160},{48,176},{64,192},{80,208},{96,224},{112... | collective-permute-start | bytes 196616 | tf_op jit(solution)/shard_map/ppermute | solution.py:147
  32.4 19.7 %all-to-all-start = ((bf16[16,32,512]{2,1,0:T(8,128)(2,1)}), bf16[16,32,512]{2,1,0:T(8,128)(2,1)S(1)}, u32[]{:S(2)}, u32[]{:S(2)}) async-start(bf16[16,32,512]{2,1,0:T(8,128)(2,1)} %broadcast_in_dim.5), calls=%async_computation | async-start | bytes 1048576 | tf_op jit(solution)/shard_map/all_to_all | solution.py:25
  52.1 6.4 %copy-start.4 = (bf16[16,32,512]{2,1,0:T(8,128)(2,1)}, bf16[16,32,512]{2,1,0:T(8,128)(2,1)S(1)}, u32[]{:S(2)}) copy-start(bf16[16,32,512]{2,1,0:T(8,128)(2,1)S(1)} %all-to-all-done) | copy-start | bytes 1572868
  52.1 1.9 %copy-start.1 = (bf16[512,1,2304]{2,0,1:T(8,128)(2,1)S(1)}, bf16[512,1,2304]{2,0,1:T(8,128)(2,1)}, u32[]{:S(2)}) copy-start(bf16[512,1,2304]{2,0,1:T(8,128)(2,1)} %param.7) | copy-start | bytes 7077892
  54.7 2.9 %collective-permute-start.9 = (bf16[256,2304]{1,0:T(8,128)(2,1)S(1)}, bf16[256,2304]{1,0:T(8,128)(2,1)S(1)}, u32[]{:S(2)}, u32[]{:S(2)}) collective-permute-start(bf16[256,2304]{1,0:T(8,128)(2,1)S(1)} %shard_map.76), channel_id=1, source_target_pairs={{0,1},{1,0},{2,3},{3,2},{4,5},{5,4},{6,7},{7,6},{8,9},{9,8},{10,11... | collective-permute-start | bytes 3538952 | tf_op jit(solution)/shard_map/ppermute | solution.py:159
  58.5 24.8 %copy-start.7 = (f32[1,2304]{1,0:T(1,128)S(1)}, f32[1,2304]{1,0:T(1,128)}, u32[]{:S(2)}) copy-start(f32[1,2304]{1,0:T(1,128)} %bias_ref.1) | copy-start | bytes 27652
  83.3 21.0 %copy-start.2 = (bf16[512,1,2304]{2,0,1:T(8,128)(2,1)S(1)}, bf16[512,1,2304]{2,0,1:T(8,128)(2,1)}, u32[]{:S(2)}) copy-start(bf16[512,1,2304]{2,0,1:T(8,128)(2,1)} %param.7) | copy-start | bytes 7077892
  104.3 2.8 %collective-permute-start.10 = (bf16[256,2304]{1,0:T(8,128)(2,1)S(1)}, bf16[256,2304]{1,0:T(8,128)(2,1)S(1)}, u32[]{:S(2)}, u32[]{:S(2)}) collective-permute-start(bf16[256,2304]{1,0:T(8,128)(2,1)S(1)} %bitcast.71), channel_id=1, source_target_pairs={{0,1},{1,0},{2,3},{3,2},{4,5},{5,4},{6,7},{7,6},{8,9},{9,8},{10,11... | collective-permute-start | bytes 3538952 | tf_op jit(solution)/shard_map/ppermute | solution.py:177
  107.1 1.1 copy-start.6
  108.2 0.8 copy-start.5
  108.9 20.9 %all-to-all-start.3 = ((bf16[16,32,512]{2,1,0:T(8,128)(2,1)}), bf16[16,32,512]{2,1,0:T(8,128)(2,1)}, u32[]{:S(2)}, u32[]{:S(2)}) async-start(bf16[16,32,512]{2,1,0:T(8,128)(2,1)} %bitcast.78), calls=%async_computation.3 | async-start | bytes 1048576 | tf_op jit(solution)/shard_map/all_to_all | solution.py:196
  129.8 22.4 %copy-start.3 = (bf16[512,1,2304]{0,2,1:T(8,128)(2,1)S(1)}, bf16[512,1,2304]{0,2,1:T(8,128)(2,1)}, u32[]{:S(2)}) copy-start(bf16[512,1,2304]{0,2,1:T(8,128)(2,1)} %copy.8) | copy-start | bytes 7077892
  131.1 23.7 %copy-start.8 = (f32[32,512]{1,0:T(8,128)}, f32[32,512]{1,0:T(8,128)S(1)}, u32[]{:S(2)}) copy-start(f32[32,512]{1,0:T(8,128)S(1)} %convert_reduce_fusion) | copy-start | bytes 196612

commit v5 on v4

--- a/solution.py
+++ b/solution.py
@@ -26,9 +26,8 @@
 
 
 SMALL = pl.BlockSpec(memory_space=pltpu.SMEM)
-STORED = pl.BlockSpec(memory_space=pltpu.HBM)
 NT = (((1,), (1,)), ((), ()))
-PIECES = 3
+TN = (((0,), (0,)), ((), ()))
 
 
 def shape(dims, dtype):
@@ -43,18 +42,17 @@
 
 def simple(kernel, out_shape, flops, moved, *operands):
     specs = [whole(operand) for operand in operands]
-    return call(kernel, out_shape, whole(out_shape), specs, [], flops, moved, *operands)
-
-
-def call(kernel, out_shape, out_spec, specs, scratch, flops, moved, *operands, room=20):
+    return call(kernel, out_shape, whole(out_shape), specs, flops, moved, *operands)
+
+
+def call(kernel, out_shape, out_spec, specs, flops, moved, *operands, steps=1):
     return pl.pallas_call(
         kernel,
         out_shape=out_shape,
-        grid=(1,),
+        grid=(steps,),
         in_specs=specs,
         out_specs=out_spec,
-        scratch_shapes=scratch,
-        compiler_params=pltpu.CompilerParams(vmem_limit_bytes=room * 1024 * 1024),
+        compiler_params=pltpu.CompilerParams(vmem_limit_bytes=20 * 1024 * 1024),
         cost_estimate=pl.CostEstimate(flops=flops, bytes_accessed=moved, transcendentals=0),
     )(*operands)
 
@@ -97,6 +95,17 @@
     other = lax.dot_general(err_ref[...], dec_ref[...], NT, preferred_element_type=F32)
     out_ref[pl.ds(pl.multiple_of(core * half, half), half), :] = own_ref[...]
     out_ref[pl.ds(pl.multiple_of((1 - core) * half, half), half), :] = other.astype(BF16)
+
+
+def dec_kernel(core_ref, latents_ref, own_ref, other_ref, out_ref):
+    core = core_ref[0]
+    total = lax.dot_general(
+        half_of(latents_ref, core), own_ref[...], TN, preferred_element_type=F32
+    )
+    total += lax.dot_general(
+        half_of(latents_ref, 1 - core), other_ref[...], TN, preferred_element_type=F32
+    )
+    out_ref[...] = total.astype(BF16)
 
 
 def enc_kernel(acts_ref, grad_ref, out_ref):
@@ -188,32 +197,61 @@
         dec,
         back,
     )
-    err = jnp.where(
-        core == 0,
-        jnp.concatenate([err_own, err_other], 0),
-        jnp.concatenate([err_other, err_own], 0),
-    )
-    back_parts = lax.all_to_all(
-        back.reshape(16, rows, local_latents), "layer", 0, 0
-    )
-    latent_grad = jnp.sum(back_parts.astype(F32), axis=0)
+    back = back.reshape(2, 8, rows, local_latents)
+
+    def share(step):
+        return lax.dynamic_index_in_dim(back, (z + step) % 8, 1, keepdims=False)
+
+    def plus(x, step):
+        return x.astype(F32) + share(step).astype(F32)
+
+    up = lax.ppermute(share(4), "layer", Z_UP)
+    down = lax.ppermute(share(-3), "layer", Z_DOWN)
+    for step in (3, 2):
+        up = lax.ppermute(plus(up, step).astype(BF16), "layer", Z_UP)
+        down = lax.ppermute(plus(down, 1 - step).astype(BF16), "layer", Z_DOWN)
+    up = plus(up, 1).astype(BF16)
+    down = plus(down, 0)
+    arrived = (
+        lax.ppermute(column(up, 1 - x_lo), "layer", Z_ACROSS),
+        lax.ppermute(column(up, x_lo), "layer", Z_UP),
+        lax.ppermute(column(down.astype(BF16), 1 - x_lo), "layer", X_NEXT),
+    )
+    latent_grad = column(down, x_lo) + sum(x.astype(F32) for x in arrived)
     own_grad_pre = jnp.where(own_pre > 0, latent_grad, 0.0).astype(BF16)
-    dec_grad = lax.dot_general(
-        latents, err, (((0,), (0,)), ((), ())), preferred_element_type=F32
-    ).astype(BF16)
+    third = width // 3
+    dec_grad = call(
+        dec_kernel,
+        shape((local_latents, width), BF16),
+        pl.BlockSpec((local_latents, third), lambda i: (0, i)),
+        [
+            SMALL,
+            whole(latents),
+            pl.BlockSpec((half, third), lambda i: (0, i)),
+            pl.BlockSpec((half, third), lambda i: (0, i)),
+        ],
+        2 * flops,
+        3 * moved,
+        core_at,
+        latents,
+        err_own,
+        err_other,
+        steps=3,
+    )
     own_grad_pre, dec_grad = lax.optimization_barrier((own_grad_pre, dec_grad))
     grad_pre = spread(own_grad_pre, "layer").reshape(tokens, local_latents)
-    enc_grad = pl.pallas_call(
+    by_rows = pl.BlockSpec((width // 2, local_latents), lambda i: (i, 0))
+    enc_grad = call(
         enc_kernel,
-        out_shape=shape((width, local_latents), BF16),
-        grid=(2,),
-        in_specs=[pl.BlockSpec((width // 2, tokens), lambda i: (i, 0)), whole(grad_pre)],
-        out_specs=pl.BlockSpec((width // 2, local_latents), lambda i: (i, 0)),
-        compiler_params=pltpu.CompilerParams(vmem_limit_bytes=16 * 1024 * 1024),
-        cost_estimate=pl.CostEstimate(
-            flops=2 * tokens * width * local_latents, bytes_accessed=3 * moved, transcendentals=0
-        ),
-    )(acts_t, grad_pre)
+        shape((width, local_latents), BF16),
+        by_rows,
+        [pl.BlockSpec((width // 2, tokens), lambda i: (i, 0)), whole(grad_pre)],
+        2 * flops,
+        3 * moved,
+        acts_t,
+        grad_pre,
+        steps=2,
+    )
     return (
         latent_grad,
         enc_grad.reshape(layers_here, width, local_latents),

time: 156 us -> 153 us (0.981)
  matrix products: 8.81 us -> 4.12 us
  starting transfers between devices: 27.5 us -> 31.9 us
  blocking collectives: 65.8 us -> 62.6 us
  Pallas kernels: 5.95 us -> 9.04 us
  other arithmetic: 2.86 us -> 0.86 us
    ppermute x0 -> x7, waiting for transfers between devices: none -> 12 us  [the longest x2 6.47 us: local(): up = lax.ppermute(plus(up, step).astype(BF16), 'layer', Z_UP)]
    all_to_all x1 -> x0, waiting for transfers between devices: 11.4 us -> none  [local(): lax.all_to_all(back.reshape(16, rows, local_latents), 'layer', 0, 0)]
    ppermute x0 -> x7, starting transfers between devices: none -> 7.68 us  [the longest x2 3.83 us: local(): down = lax.ppermute(plus(down, 1 - step).astype(BF16), 'layer', Z_DOWN)]
    all_to_all x1 -> x0, starting transfers between devices: 4.83 us -> none  [local(): lax.all_to_all(back.reshape(16, rows, local_latents), 'layer', 0, 0)]
    dot_general x1 -> x0, matrix products: 4.69 us -> none  [local(): lax.dot_general(latents, err, (((0,), (0,)), ((), ())), preferred_element...]
    all_to_all x1, blocking collectives: 20.2 us -> 17.1 us  [spread(): return lax.all_to_all(copies, axis, 0, 0, axis_index_groups=groups)]
    pallas_call x6 -> x7, Pallas kernels: 5.95 us -> 9.04 us  [call(): pl.pallas_call(kernel, out_shape=out_shape, grid=(steps,), in_specs=specs...]
    ppermute x1 -> x2, starting transfers between devices: 0.08 us -> 1.67 us  [local(): lax.ppermute(column(up, 1 - x_lo), 'layer', Z_ACROSS)]
  transfers between devices with their start and end apart: 13 -> 21, of which waited for: 11 -> 15; matrix products, arithmetic and copies ran while one was open for 9% -> 7% of each run, Pallas kernels for 1% -> 3%
where the time goes in v5:
time: 153 us; the launch traced here: 152 us
  blocking collectives  62.6 us (41%)
  starting transfers between devices  31.9 us (21%)
  waiting for transfers between devices  31.3 us (20%)
  local copies, waits for them, and re-layouts  11.2 us (7%)
  Pallas kernels  9.04 us (6%)
  matrix products  4.12 us (3%)
    all_to_all x1, blocking collectives, local(): lax.all_to_all(chip_sum.reshape(8, rows, width), 'latent', 0, 0, axis_ind...  24.8 us
    all_to_all x1, blocking collectives, local(): lax.all_to_all(err_copies, 'latent', 0, 0, axis_index_groups=CHIP_GROUPS)  20.8 us
    all_to_all x1, blocking collectives, spread(): return lax.all_to_all(copies, axis, 0, 0, axis_index_groups=groups)  17.1 us
    pallas_call x7, Pallas kernels, call(): pl.pallas_call(kernel, out_shape=out_shape, grid=(steps,), in_specs=specs...  9.04 us
    all_to_all x1, starting transfers between devices, spread(): return lax.all_to_all(copies, axis, 0, 0, axis_index_groups=groups)  8.21 us
    unnamed x13, local copies, waits for them, and re-layouts  6.49 us
    ppermute x2, waiting for transfers between devices, local(): up = lax.ppermute(plus(up, step).astype(BF16), 'layer', Z_UP)  6.47 us
    all_to_all x1, waiting for transfers between devices, spread(): return lax.all_to_all(copies, axis, 0, 0, axis_index_groups=groups)  6.28 us
  transfers between devices with their start and end apart: 21, of which 15 were waited for; matrix products, arithmetic and copies ran while one was open for 7% of the time, Pallas kernels for 3%

profile of v5, /device:TPU:34, one launch (start us, length us, event | category | flops | bytes accessed | tf_op | source)
XLA Modules:
  0.0 152.0 jit_solution(17333277193800173452)
XLA Ops:
  3.5 2.0 %collective-permute-start.3 = (f32[64,512]{1,0:T(8,128)S(1)}, f32[64,512]{1,0:T(8,128)S(1)}, u32[]{:S(2)}, u32[]{:S(2)}) collective-permute-start(f32[64,512]{1,0:T(8,128)S(1)} %fusion.14), channel_id=1, source_target_pairs={{0,16},{16,32},{32,48},{48,64},{64,80},{80,96},{96,112},{112,0},{1... | collective-permute-start | bytes 393224 | tf_op jit(solution)/shard_map/ppermute | solution.py:142
  9.4 2.0 %collective-permute-start.4 = (f32[64,512]{1,0:T(8,128)S(1)}, f32[64,512]{1,0:T(8,128)S(1)}, u32[]{:S(2)}, u32[]{:S(2)}) collective-permute-start(f32[64,512]{1,0:T(8,128)S(1)} %fusion.19), channel_id=1, source_target_pairs={{0,16},{16,32},{32,48},{48,64},{64,80},{80,96},{96,112},{112,0},{1... | collective-permute-start | bytes 393224 | tf_op jit(solution)/shard_map/ppermute | solution.py:144
  11.9 2.4 %collective-permute-start.1 = (f32[64,512]{1,0:T(8,128)S(1)}, f32[64,512]{1,0:T(8,128)S(1)}, u32[]{:S(2)}, u32[]{:S(2)}) collective-permute-start(f32[64,512]{1,0:T(8,128)S(1)} %fusion.16), channel_id=1, source_target_pairs={{16,0},{32,16},{48,32},{64,48},{80,64},{96,80},{112,96},{0,112},{1... | collective-permute-start | bytes 393224 | tf_op jit(solution)/shard_map/ppermute | solution.py:144
  14.8 1.8 %collective-permute-done.4 = f32[64,512]{1,0:T(8,128)S(1)} collective-permute-done((f32[64,512]{1,0:T(8,128)S(1)}, f32[64,512]{1,0:T(8,128)S(1)}, u32[]{:S(2)}, u32[]{:S(2)}) %collective-permute-start.4) | collective-permute-done | bytes 131104 | tf_op jit(solution)/shard_map/ppermute | solution.py:144
  17.5 2.6 %collective-permute-start.2 = (f32[64,512]{1,0:T(8,128)S(1)}, f32[64,512]{1,0:T(8,128)S(1)}, u32[]{:S(2)}, u32[]{:S(2)}) collective-permute-start(f32[64,512]{1,0:T(8,128)S(1)} %add.201), channel_id=1, source_target_pairs={{16,0},{32,16},{48,32},{64,48},{80,64},{96,80},{112,96},{0,112},{1... | collective-permute-start | bytes 393224 | tf_op jit(solution)/shard_map/ppermute | solution.py:146
  20.7 2.2 %collective-permute-done.5 = f32[64,512]{1,0:T(8,128)S(1)} collective-permute-done((f32[64,512]{1,0:T(8,128)S(1)}, f32[64,512]{1,0:T(8,128)S(1)}, u32[]{:S(2)}, u32[]{:S(2)}) %collective-permute-start.5) | collective-permute-done | bytes 131104 | tf_op jit(solution)/shard_map/ppermute | solution.py:146
  23.0 3.5 %collective-permute-start.7 = (f32[32,512]{1,0:T(8,128)S(1)}, f32[32,512]{1,0:T(8,128)S(1)}, u32[]{:S(2)}, u32[]{:S(2)}) collective-permute-start(f32[32,512]{1,0:T(8,128)S(1)} %get-tuple-element.37), channel_id=1, source_target_pairs={{0,16},{16,32},{32,48},{48,64},{64,80},{80,96},{96,112},{112,0},{1... | collective-permute-start | bytes 196616 | tf_op jit(solution)/shard_map/ppermute | solution.py:155
  29.2 1.7 %collective-permute-done.8 = f32[32,512]{1,0:T(8,128)S(1)} collective-permute-done((f32[32,512]{1,0:T(8,128)S(1)}, f32[32,512]{1,0:T(8,128)S(1)}, u32[]{:S(2)}, u32[]{:S(2)}) %collective-permute-start.8) | collective-permute-done | bytes 65568 | tf_op jit(solution)/shard_map/ppermute | solution.py:156
  31.8 8.2 %all-to-all-start = ((bf16[16,32,512]{2,1,0:T(8,128)(2,1)}), bf16[16,32,512]{2,1,0:T(8,128)(2,1)S(1)}, u32[]{:S(2)}, u32[]{:S(2)}) async-start(bf16[16,32,512]{2,1,0:T(8,128)(2,1)} %broadcast_in_dim.5), calls=%async_computation | async-start | bytes 1048576 | tf_op jit(solution)/shard_map/all_to_all | solution.py:25
  40.0 4.3 %copy.8 = bf16[512,1,2304]{0,2,1:T(8,128)(2,1)} copy(bf16[512,1,2304]{2,0,1:T(8,128)(2,1)} %param.5) | data formatting | bytes 4718592 | tf_op args[0]
  45.2 6.3 %all-to-all-done = bf16[16,32,512]{2,1,0:T(8,128)(2,1)S(1)} async-done(((bf16[16,32,512]{2,1,0:T(8,128)(2,1)}), bf16[16,32,512]{2,1,0:T(8,128)(2,1)S(1)}, u32[]{:S(2)}, u32[]{:S(2)}) %all-to-all-start) | async-done | bytes 524320 | tf_op jit(solution)/shard_map/all_to_all | solution.py:25
  54.0 2.8 %collective-permute-done.9.received_ref = bf16[256,2304]{1,0:T(8,128)(2,1)S(1)} collective-permute-done((bf16[256,2304]{1,0:T(8,128)(2,1)S(1)}, bf16[256,2304]{1,0:T(8,128)(2,1)S(1)}, u32[]{:S(2)}, u32[]{:S(2)}) %collective-permute-start.9) | collective-permute-done | bytes 1179680 | tf_op jit(solution)/shard_map/ppermute | solution.py:168
  57.7 24.8 %all_to_all.20.shares_ref = bf16[8,32,2304]{2,1,0:T(8,128)(2,1)S(1)} all-to-all(bf16[8,32,2304]{2,1,0:T(8,128)(2,1)S(1)} %bitcast.115), channel_id=1, replica_groups={{0,2,4,6,8,10,12,14},{1,3,5,7,9,11,13,15},{16,18,20,22,24,26,28,30},{17..., dimensions={0} | all-to-all | bytes 2359296 | tf_op jit(solution)/shard_map/all_to_all | solution.py:170
  82.7 20.8 %all_to_all.21 = bf16[8,32,2304]{2,1,0:T(8,128)(2,1)S(1)} all-to-all(bf16[8,32,2304]{2,1,0:T(8,128)(2,1)S(1)} %shard_map.78), channel_id=1, replica_groups={{0,2,4,6,8,10,12,14},{1,3,5,7,9,11,13,15},{16,18,20,22,24,26,28,30},{17..., dimensions={0} | all-to-all | bytes 2359296 | tf_op jit(solution)/shard_map/all_to_all | solution.py:183
  104.3 2.0 %collective-permute-done.10.err_ref.other_ref = bf16[256,2304]{1,0:T(8,128)(2,1)S(1)} collective-permute-done((bf16[256,2304]{1,0:T(8,128)(2,1)S(1)}, bf16[256,2304]{1,0:T(8,128)(2,1)S(1)}, u32[]{:S(2)}, u32[]{:S(2)}) %collective-permute-start.10) | collective-permute-done | bytes 1179680 | tf_op jit(solution)/shard_map/ppermute | solution.py:186
  107.2 2.0 %collective-permute-start.11 = (bf16[2,32,512]{2,1,0:T(8,128)(2,1)S(1)}, bf16[2,32,512]{2,1,0:T(8,128)(2,1)S(1)}, u32[]{:S(2)}, u32[]{:S(2)}) collective-permute-start(bf16[2,32,512]{2,1,0:T(8,128)(2,1)S(1)} %get-tuple-element.36), channel_id=1, source_target_pairs={{16,0},{32,16},{48,32},{64,48},{80,64},{96,80},{112,96},{0,112},{1... | collective-permute-start | bytes 196616 | tf_op jit(solution)/shard_map/ppermute | solution.py:209
  109.2 2.2 %collective-permute-done.14 = bf16[2,32,512]{2,1,0:T(8,128)(2,1)S(1)} collective-permute-done((bf16[2,32,512]{2,1,0:T(8,128)(2,1)S(1)}, bf16[2,32,512]{2,1,0:T(8,128)(2,1)S(1)}, u32[]{:S(2)}, u32[]{:S(2)}) %collective-permute-start.14) | collective-permute-done | bytes 65568 | tf_op jit(solution)/shard_map/ppermute | solution.py:208
  111.7 4.1 %collective-permute-done.15 = bf16[2,32,512]{2,1,0:T(8,128)(2,1)S(1)} collective-permute-done((bf16[2,32,512]{2,1,0:T(8,128)(2,1)S(1)}, bf16[2,32,512]{2,1,0:T(8,128)(2,1)S(1)}, u32[]{:S(2)}, u32[]{:S(2)}) %collective-permute-start.15) | collective-permute-done | bytes 65568 | tf_op jit(solution)/shard_map/ppermute | solution.py:211
  115.9 2.5 %collective-permute-start.12 = (bf16[2,32,512]{2,1,0:T(8,128)(2,1)S(1)}, bf16[2,32,512]{2,1,0:T(8,128)(2,1)S(1)}, u32[]{:S(2)}, u32[]{:S(2)}) collective-permute-start(bf16[2,32,512]{2,1,0:T(8,128)(2,1)S(1)} %get-tuple-element.34), channel_id=1, source_target_pairs={{16,0},{32,16},{48,32},{64,48},{80,64},{96,80},{112,96},{0,112},{1... | collective-permute-start | bytes 196616 | tf_op jit(solution)/shard_map/ppermute | solution.py:212
  118.3 1.9 %collective-permute-done.12 = bf16[2,32,512]{2,1,0:T(8,128)(2,1)S(1)} collective-permute-done((bf16[2,32,512]{2,1,0:T(8,128)(2,1)S(1)}, bf16[2,32,512]{2,1,0:T(8,128)(2,1)S(1)}, u32[]{:S(2)}, u32[]{:S(2)}) %collective-permute-start.12) | collective-permute-done | bytes 65568 | tf_op jit(solution)/shard_map/ppermute | solution.py:212
  120.2 2.4 %collective-permute-done.16 = bf16[2,32,512]{2,1,0:T(8,128)(2,1)S(1)} collective-permute-done((bf16[2,32,512]{2,1,0:T(8,128)(2,1)S(1)}, bf16[2,32,512]{2,1,0:T(8,128)(2,1)S(1)}, u32[]{:S(2)}, u32[]{:S(2)}) %collective-permute-start.16) | collective-permute-done | bytes 65568 | tf_op jit(solution)/shard_map/ppermute | solution.py:211
  128.5 3.1 %shard_map.81 = bf16[512,2304]{1,0:T(8,128)(2,1)} custom-call(s32[1]{0:T(128)} %bitcast.core_ref, bf16[512,512]{1,0:T(8,128)(2,1)S(1)} %bitcast.114, bf16[256,2304]{1,0:T(8,128)(2,1)S(1)} %bitcast.110, bf16[256,2304]{1,0:T(8,128)(2,1)S(1)} %collective-permute-done.10.err_ref.other_ref), custom_call_target="tpu_custom_call" | custom-call | flops 1207959552 | bytes 10616832 | tf_op jit(solution)/shard_map/pallas_call | solution.py:49
  132.4 17.1 %all_to_all.22 = bf16[16,32,512]{2,1,0:T(8,128)(2,1)S(1)} all-to-all(bf16[16,32,512]{2,1,0:T(8,128)(2,1)S(1)} %broadcast_in_dim.7), channel_id=1, replica_groups=mesh['layer'=16,'latent'=16] {'layer'}, dimensions={0} | all-to-all | bytes 1048576 | tf_op jit(solution)/shard_map/all_to_all | solution.py:25
  149.5 2.6 %shard_map.82 = bf16[2304,512]{1,0:T(8,128)(2,1)} custom-call(bf16[2304,512]{1,0:T(8,128)(2,1)S(1)} %bitcast.111, bf16[512,512]{1,0:T(8,128)(2,1)S(1)} %bitcast.121), custom_call_target="tpu_custom_call" | custom-call | flops 1207959552 | bytes 10616832 | tf_op jit(solution)/shard_map/pallas_call | solution.py:49
  (69 shorter events, 25.8 us)
Async XLA Ops:
  3.5 5.3 %collective-permute-start.3 = (f32[64,512]{1,0:T(8,128)S(1)}, f32[64,512]{1,0:T(8,128)S(1)}, u32[]{:S(2)}, u32[]{:S(2)}) collective-permute-start(f32[64,512]{1,0:T(8,128)S(1)} %fusion.14), channel_id=1, source_target_pairs={{0,16},{16,32},{32,48},{48,64},{64,80},{80,96},{96,112},{112,0},{1... | collective-permute-start | bytes 393224 | tf_op jit(solution)/shard_map/ppermute | solution.py:142
  5.5 5.8 %collective-permute-start = (f32[64,512]{1,0:T(8,128)S(1)}, f32[64,512]{1,0:T(8,128)S(1)}, u32[]{:S(2)}, u32[]{:S(2)}) collective-permute-start(f32[64,512]{1,0:T(8,128)S(1)} %fusion.12), channel_id=1, source_target_pairs={{16,0},{32,16},{48,32},{64,48},{80,64},{96,80},{112,96},{0,112},{1... | collective-permute-start | bytes 393224 | tf_op jit(solution)/shard_map/ppermute | solution.py:142
  9.4 7.3 %collective-permute-start.4 = (f32[64,512]{1,0:T(8,128)S(1)}, f32[64,512]{1,0:T(8,128)S(1)}, u32[]{:S(2)}, u32[]{:S(2)}) collective-permute-start(f32[64,512]{1,0:T(8,128)S(1)} %fusion.19), channel_id=1, source_target_pairs={{0,16},{16,32},{32,48},{48,64},{64,80},{80,96},{96,112},{112,0},{1... | collective-permute-start | bytes 393224 | tf_op jit(solution)/shard_map/ppermute | solution.py:144
  11.9 5.6 %collective-permute-start.1 = (f32[64,512]{1,0:T(8,128)S(1)}, f32[64,512]{1,0:T(8,128)S(1)}, u32[]{:S(2)}, u32[]{:S(2)}) collective-permute-start(f32[64,512]{1,0:T(8,128)S(1)} %fusion.16), channel_id=1, source_target_pairs={{16,0},{32,16},{48,32},{64,48},{80,64},{96,80},{112,96},{0,112},{1... | collective-permute-start | bytes 393224 | tf_op jit(solution)/shard_map/ppermute | solution.py:144
  16.6 6.3 %collective-permute-start.5 = (f32[64,512]{1,0:T(8,128)S(1)}, f32[64,512]{1,0:T(8,128)S(1)}, u32[]{:S(2)}, u32[]{:S(2)}) collective-permute-start(f32[64,512]{1,0:T(8,128)S(1)} %add.213), channel_id=1, source_target_pairs={{0,16},{16,32},{32,48},{48,64},{64,80},{80,96},{96,112},{112,0},{1... | collective-permute-start | bytes 393224 | tf_op jit(solution)/shard_map/ppermute | solution.py:146
  17.5 9.0 %collective-permute-start.2 = (f32[64,512]{1,0:T(8,128)S(1)}, f32[64,512]{1,0:T(8,128)S(1)}, u32[]{:S(2)}, u32[]{:S(2)}) collective-permute-start(f32[64,512]{1,0:T(8,128)S(1)} %add.201), channel_id=1, source_target_pairs={{16,0},{32,16},{48,32},{64,48},{80,64},{96,80},{112,96},{0,112},{1... | collective-permute-start | bytes 393224 | tf_op jit(solution)/shard_map/ppermute | solution.py:146
  22.9 5.5 %collective-permute-start.6 = (f32[32,512]{1,0:T(8,128)S(1)}, f32[32,512]{1,0:T(8,128)S(1)}, u32[]{:S(2)}, u32[]{:S(2)}) collective-permute-start(f32[32,512]{1,0:T(8,128)S(1)} %get-tuple-element.38), channel_id=1, source_target_pairs={{0,144},{16,160},{32,176},{48,192},{64,208},{80,224},{96,240},{112... | collective-permute-start | bytes 196616 | tf_op jit(solution)/shard_map/ppermute | solution.py:154
  23.0 6.2 %collective-permute-start.7 = (f32[32,512]{1,0:T(8,128)S(1)}, f32[32,512]{1,0:T(8,128)S(1)}, u32[]{:S(2)}, u32[]{:S(2)}) collective-permute-start(f32[32,512]{1,0:T(8,128)S(1)} %get-tuple-element.37), channel_id=1, source_target_pairs={{0,16},{16,32},{32,48},{48,64},{64,80},{80,96},{96,112},{112,0},{1... | collective-permute-start | bytes 196616 | tf_op jit(solution)/shard_map/ppermute | solution.py:155
  26.6 4.4 %collective-permute-start.8 = (f32[32,512]{1,0:T(8,128)S(1)}, f32[32,512]{1,0:T(8,128)S(1)}, u32[]{:S(2)}, u32[]{:S(2)}) collective-permute-start(f32[32,512]{1,0:T(8,128)S(1)} %dynamic-slice_bitcast_fusion.3), channel_id=1, source_target_pairs={{0,128},{16,144},{32,160},{48,176},{64,192},{80,208},{96,224},{112... | collective-permute-start | bytes 196616 | tf_op jit(solution)/shard_map/ppermute | solution.py:156
  31.8 19.7 %all-to-all-start = ((bf16[16,32,512]{2,1,0:T(8,128)(2,1)}), bf16[16,32,512]{2,1,0:T(8,128)(2,1)S(1)}, u32[]{:S(2)}, u32[]{:S(2)}) async-start(bf16[16,32,512]{2,1,0:T(8,128)(2,1)} %broadcast_in_dim.5), calls=%async_computation | async-start | bytes 1048576 | tf_op jit(solution)/shard_map/all_to_all | solution.py:25
  53.9 2.9 %collective-permute-start.9 = (bf16[256,2304]{1,0:T(8,128)(2,1)S(1)}, bf16[256,2304]{1,0:T(8,128)(2,1)S(1)}, u32[]{:S(2)}, u32[]{:S(2)}) collective-permute-start(bf16[256,2304]{1,0:T(8,128)(2,1)S(1)} %shard_map.76), channel_id=1, source_target_pairs={{0,1},{1,0},{2,3},{3,2},{4,5},{5,4},{6,7},{7,6},{8,9},{9,8},{10,11... | collective-permute-start | bytes 3538952 | tf_op jit(solution)/shard_map/ppermute | solution.py:168
  57.6 24.8 %copy-start.4 = (f32[1,2304]{1,0:T(1,128)S(1)}, f32[1,2304]{1,0:T(1,128)}, u32[]{:S(2)}) copy-start(f32[1,2304]{1,0:T(1,128)} %bias_ref.1) | copy-start | bytes 27652
  82.5 21.0 %copy-start.2 = (bf16[512,1,2304]{2,0,1:T(8,128)(2,1)S(1)}, bf16[512,1,2304]{2,0,1:T(8,128)(2,1)}, u32[]{:S(2)}) copy-start(bf16[512,1,2304]{2,0,1:T(8,128)(2,1)} %param.7) | copy-start | bytes 7077892
  103.4 2.8 %collective-permute-start.10 = (bf16[256,2304]{1,0:T(8,128)(2,1)S(1)}, bf16[256,2304]{1,0:T(8,128)(2,1)S(1)}, u32[]{:S(2)}, u32[]{:S(2)}) collective-permute-start(bf16[256,2304]{1,0:T(8,128)(2,1)S(1)} %bitcast.108), channel_id=1, source_target_pairs={{0,1},{1,0},{2,3},{3,2},{4,5},{5,4},{6,7},{7,6},{8,9},{9,8},{10,11... | collective-permute-start | bytes 3538952 | tf_op jit(solution)/shard_map/ppermute | solution.py:186
  107.1 4.3 %collective-permute-start.14 = (bf16[2,32,512]{2,1,0:T(8,128)(2,1)S(1)}, bf16[2,32,512]{2,1,0:T(8,128)(2,1)S(1)}, u32[]{:S(2)}, u32[]{:S(2)}) collective-permute-start(bf16[2,32,512]{2,1,0:T(8,128)(2,1)S(1)} %get-tuple-element.35), channel_id=1, source_target_pairs={{0,16},{16,32},{32,48},{48,64},{64,80},{80,96},{96,112},{112,0},{1... | collective-permute-start | bytes 196616 | tf_op jit(solution)/shard_map/ppermute | solution.py:208
  107.2 4.5 %collective-permute-start.11 = (bf16[2,32,512]{2,1,0:T(8,128)(2,1)S(1)}, bf16[2,32,512]{2,1,0:T(8,128)(2,1)S(1)}, u32[]{:S(2)}, u32[]{:S(2)}) collective-permute-start(bf16[2,32,512]{2,1,0:T(8,128)(2,1)S(1)} %get-tuple-element.36), channel_id=1, source_target_pairs={{16,0},{32,16},{48,32},{64,48},{80,64},{96,80},{112,96},{0,112},{1... | collective-permute-start | bytes 196616 | tf_op jit(solution)/shard_map/ppermute | solution.py:209
  111.5 4.3 %collective-permute-start.15 = (bf16[2,32,512]{2,1,0:T(8,128)(2,1)S(1)}, bf16[2,32,512]{2,1,0:T(8,128)(2,1)S(1)}, u32[]{:S(2)}, u32[]{:S(2)}) collective-permute-start(bf16[2,32,512]{2,1,0:T(8,128)(2,1)S(1)} %fusion.24), channel_id=1, source_target_pairs={{0,16},{16,32},{32,48},{48,64},{64,80},{80,96},{96,112},{112,0},{1... | collective-permute-start | bytes 196616 | tf_op jit(solution)/shard_map/ppermute | solution.py:211
  115.9 4.4 %collective-permute-start.12 = (bf16[2,32,512]{2,1,0:T(8,128)(2,1)S(1)}, bf16[2,32,512]{2,1,0:T(8,128)(2,1)S(1)}, u32[]{:S(2)}, u32[]{:S(2)}) collective-permute-start(bf16[2,32,512]{2,1,0:T(8,128)(2,1)S(1)} %get-tuple-element.34), channel_id=1, source_target_pairs={{16,0},{32,16},{48,32},{64,48},{80,64},{96,80},{112,96},{0,112},{1... | collective-permute-start | bytes 196616 | tf_op jit(solution)/shard_map/ppermute | solution.py:212
  118.3 4.3 %collective-permute-start.16 = (bf16[2,32,512]{2,1,0:T(8,128)(2,1)S(1)}, bf16[2,32,512]{2,1,0:T(8,128)(2,1)S(1)}, u32[]{:S(2)}, u32[]{:S(2)}) collective-permute-start(bf16[2,32,512]{2,1,0:T(8,128)(2,1)S(1)} %get-tuple-element.33), channel_id=1, source_target_pairs={{0,16},{16,32},{32,48},{48,64},{64,80},{80,96},{96,112},{112,0},{1... | collective-permute-start | bytes 196616 | tf_op jit(solution)/shard_map/ppermute | solution.py:211
  122.6 4.3 %collective-permute-start.13 = (bf16[2,32,512]{2,1,0:T(8,128)(2,1)S(1)}, bf16[2,32,512]{2,1,0:T(8,128)(2,1)S(1)}, u32[]{:S(2)}, u32[]{:S(2)}) collective-permute-start(bf16[2,32,512]{2,1,0:T(8,128)(2,1)S(1)} %get-tuple-element.32), channel_id=1, source_target_pairs={{16,0},{32,16},{48,32},{64,48},{80,64},{96,80},{112,96},{0,112},{1... | collective-permute-start | bytes 196616 | tf_op jit(solution)/shard_map/ppermute | solution.py:212
  124.0 7.6 %collective-permute-start.17 = (bf16[32,512]{1,0:T(8,128)(2,1)S(1)}, bf16[32,512]{1,0:T(8,128)(2,1)S(1)}, u32[]{:S(2)}, u32[]{:S(2)}) collective-permute-start(bf16[32,512]{1,0:T(8,128)(2,1)S(1)} %get-tuple-element.39), channel_id=1, source_target_pairs={{0,144},{16,160},{32,176},{48,192},{64,208},{80,224},{96,240},{112... | collective-permute-start | bytes 98312 | tf_op jit(solution)/shard_map/ppermute | solution.py:216
  125.6 6.0 %collective-permute-start.18 = (bf16[32,512]{1,0:T(8,128)(2,1)S(1)}, bf16[32,512]{1,0:T(8,128)(2,1)S(1)}, u32[]{:S(2)}, u32[]{:S(2)}) collective-permute-start(bf16[32,512]{1,0:T(8,128)(2,1)S(1)} %get-tuple-element.40), channel_id=1, source_target_pairs={{0,16},{16,32},{32,48},{48,64},{64,80},{80,96},{96,112},{112,0},{1... | collective-permute-start | bytes 98312 | tf_op jit(solution)/shard_map/ppermute | solution.py:217
  127.0 22.4 %copy-start.3 = (bf16[512,1,2304]{0,2,1:T(8,128)(2,1)S(1)}, bf16[512,1,2304]{0,2,1:T(8,128)(2,1)}, u32[]{:S(2)}) copy-start(bf16[512,1,2304]{0,2,1:T(8,128)(2,1)} %copy.8) | copy-start | bytes 7077892
  127.0 4.6 %collective-permute-start.19 = (bf16[32,512]{1,0:T(8,128)(2,1)S(1)}, bf16[32,512]{1,0:T(8,128)(2,1)S(1)}, u32[]{:S(2)}, u32[]{:S(2)}) collective-permute-start(bf16[32,512]{1,0:T(8,128)(2,1)S(1)} %fusion.28), channel_id=1, source_target_pairs={{0,128},{16,144},{32,160},{48,176},{64,192},{80,208},{96,224},{112... | collective-permute-start | bytes 98312 | tf_op jit(solution)/shard_map/ppermute | solution.py:218
  (3 other events, 19.6 us)

commit v6 on v5

--- a/solution.py
+++ b/solution.py
@@ -137,8 +137,8 @@
         block = lax.dynamic_index_in_dim(tall, (z + step) % 8, 1, keepdims=False)
         return jnp.dot(block.reshape(2 * rows, width), enc, preferred_element_type=F32)
 
-    up, down = partial(4), partial(-3)
-    up, down, tall = lax.optimization_barrier((up, down, tall))
+    up, tall = lax.optimization_barrier((partial(4), tall))
+    down = partial(-3)
     up, down = lax.ppermute(up, "layer", Z_UP), lax.ppermute(down, "layer", Z_DOWN)
     up, down = up + partial(3), down + partial(-2)
     up, down = lax.ppermute(up, "layer", Z_UP), lax.ppermute(down, "layer", Z_DOWN)

time: 153 us -> 152 us (level)
    ppermute x3, waiting for transfers between devices: 0.75 us -> 3.74 us  [local(): lax.ppermute(down, 'layer', Z_DOWN)]
    ppermute x3, waiting for transfers between devices: 4.62 us -> 1.67 us  [local(): lax.ppermute(up, 'layer', Z_UP)]
where the time goes in v6:
time: 152 us
  blocking collectives  62.7 us (41%)
  waiting for transfers between devices  31.7 us (21%)
  starting transfers between devices  31.4 us (21%)
  local copies, waits for them, and re-layouts  11.2 us (7%)
  Pallas kernels  9.05 us (6%)
  matrix products  4.11 us (3%)
    all_to_all x1, blocking collectives, local(): lax.all_to_all(chip_sum.reshape(8, rows, width), 'latent', 0, 0, axis_ind...  24.7 us
    all_to_all x1, blocking collectives, local(): lax.all_to_all(err_copies, 'latent', 0, 0, axis_index_groups=CHIP_GROUPS)  20.8 us
    all_to_all x1, blocking collectives, spread(): return lax.all_to_all(copies, axis, 0, 0, axis_index_groups=groups)  17.2 us
    pallas_call x7, Pallas kernels, call(): pl.pallas_call(kernel, out_shape=out_shape, grid=(steps,), in_specs=specs...  9.05 us
    all_to_all x1, starting transfers between devices, spread(): return lax.all_to_all(copies, axis, 0, 0, axis_index_groups=groups)  8.53 us
    unnamed x13, local copies, waits for them, and re-layouts  6.54 us
    ppermute x2, waiting for transfers between devices, local(): up = lax.ppermute(plus(up, step).astype(BF16), 'layer', Z_UP)  6.41 us
    all_to_all x1, waiting for transfers between devices, spread(): return lax.all_to_all(copies, axis, 0, 0, axis_index_groups=groups)  6.37 us
  transfers between devices with their start and end apart: 21, of which 15 were waited for; matrix products, arithmetic and copies ran while one was open for 7% of the time, Pallas kernels for 3%

profile of v6, /device:TPU:34, one launch (start us, length us, event | category | flops | bytes accessed | tf_op | source)
XLA Modules:
  0.0 151.9 jit_solution(3078225231651153490)
XLA Ops:
  2.9 2.0 %collective-permute-start.3 = (f32[64,512]{1,0:T(8,128)S(1)}, f32[64,512]{1,0:T(8,128)S(1)}, u32[]{:S(2)}, u32[]{:S(2)}) collective-permute-start(f32[64,512]{1,0:T(8,128)S(1)} %fusion.14), channel_id=1, source_target_pairs={{0,16},{16,32},{32,48},{48,64},{64,80},{80,96},{96,112},{112,0},{1... | collective-permute-start | bytes 393224 | tf_op jit(solution)/shard_map/ppermute | solution.py:142
  8.8 2.0 %collective-permute-start.4 = (f32[64,512]{1,0:T(8,128)S(1)}, f32[64,512]{1,0:T(8,128)S(1)}, u32[]{:S(2)}, u32[]{:S(2)}) collective-permute-start(f32[64,512]{1,0:T(8,128)S(1)} %fusion.19), channel_id=1, source_target_pairs={{0,16},{16,32},{32,48},{48,64},{64,80},{80,96},{96,112},{112,0},{1... | collective-permute-start | bytes 393224 | tf_op jit(solution)/shard_map/ppermute | solution.py:144
  12.8 1.9 %collective-permute-start.1 = (f32[64,512]{1,0:T(8,128)S(1)}, f32[64,512]{1,0:T(8,128)S(1)}, u32[]{:S(2)}, u32[]{:S(2)}) collective-permute-start(f32[64,512]{1,0:T(8,128)S(1)} %fusion.16), channel_id=1, source_target_pairs={{16,0},{32,16},{48,32},{64,48},{80,64},{96,80},{112,96},{0,112},{1... | collective-permute-start | bytes 393224 | tf_op jit(solution)/shard_map/ppermute | solution.py:144
  16.7 2.3 %collective-permute-done.1 = f32[64,512]{1,0:T(8,128)S(1)} collective-permute-done((f32[64,512]{1,0:T(8,128)S(1)}, f32[64,512]{1,0:T(8,128)S(1)}, u32[]{:S(2)}, u32[]{:S(2)}) %collective-permute-start.1) | collective-permute-done | bytes 131104 | tf_op jit(solution)/shard_map/ppermute | solution.py:144
  19.0 2.1 %collective-permute-start.2 = (f32[64,512]{1,0:T(8,128)S(1)}, f32[64,512]{1,0:T(8,128)S(1)}, u32[]{:S(2)}, u32[]{:S(2)}) collective-permute-start(f32[64,512]{1,0:T(8,128)S(1)} %add.201), channel_id=1, source_target_pairs={{16,0},{32,16},{48,32},{64,48},{80,64},{96,80},{112,96},{0,112},{1... | collective-permute-start | bytes 393224 | tf_op jit(solution)/shard_map/ppermute | solution.py:146
  22.7 3.3 %collective-permute-start.7 = (f32[32,512]{1,0:T(8,128)S(1)}, f32[32,512]{1,0:T(8,128)S(1)}, u32[]{:S(2)}, u32[]{:S(2)}) collective-permute-start(f32[32,512]{1,0:T(8,128)S(1)} %get-tuple-element.34), channel_id=1, source_target_pairs={{0,16},{16,32},{32,48},{48,64},{64,80},{80,96},{96,112},{112,0},{1... | collective-permute-start | bytes 196616 | tf_op jit(solution)/shard_map/ppermute | solution.py:155
  28.6 1.8 %collective-permute-done.8 = f32[32,512]{1,0:T(8,128)S(1)} collective-permute-done((f32[32,512]{1,0:T(8,128)S(1)}, f32[32,512]{1,0:T(8,128)S(1)}, u32[]{:S(2)}, u32[]{:S(2)}) %collective-permute-start.8) | collective-permute-done | bytes 65568 | tf_op jit(solution)/shard_map/ppermute | solution.py:156
  31.3 8.5 %all-to-all-start = ((bf16[16,32,512]{2,1,0:T(8,128)(2,1)}), bf16[16,32,512]{2,1,0:T(8,128)(2,1)S(1)}, u32[]{:S(2)}, u32[]{:S(2)}) async-start(bf16[16,32,512]{2,1,0:T(8,128)(2,1)} %broadcast_in_dim.5), calls=%async_computation | async-start | bytes 1048576 | tf_op jit(solution)/shard_map/all_to_all | solution.py:25
  39.8 4.3 %copy.8 = bf16[512,1,2304]{0,2,1:T(8,128)(2,1)} copy(bf16[512,1,2304]{2,0,1:T(8,128)(2,1)} %param.5) | data formatting | bytes 4718592 | tf_op args[0]
  45.0 6.4 %all-to-all-done = bf16[16,32,512]{2,1,0:T(8,128)(2,1)S(1)} async-done(((bf16[16,32,512]{2,1,0:T(8,128)(2,1)}), bf16[16,32,512]{2,1,0:T(8,128)(2,1)S(1)}, u32[]{:S(2)}, u32[]{:S(2)}) %all-to-all-start) | async-done | bytes 524320 | tf_op jit(solution)/shard_map/all_to_all | solution.py:25
  53.9 2.8 %collective-permute-done.9.received_ref = bf16[256,2304]{1,0:T(8,128)(2,1)S(1)} collective-permute-done((bf16[256,2304]{1,0:T(8,128)(2,1)S(1)}, bf16[256,2304]{1,0:T(8,128)(2,1)S(1)}, u32[]{:S(2)}, u32[]{:S(2)}) %collective-permute-start.9) | collective-permute-done | bytes 1179680 | tf_op jit(solution)/shard_map/ppermute | solution.py:168
  57.6 24.7 %all_to_all.20.shares_ref = bf16[8,32,2304]{2,1,0:T(8,128)(2,1)S(1)} all-to-all(bf16[8,32,2304]{2,1,0:T(8,128)(2,1)S(1)} %bitcast.115), channel_id=1, replica_groups={{0,2,4,6,8,10,12,14},{1,3,5,7,9,11,13,15},{16,18,20,22,24,26,28,30},{17..., dimensions={0} | all-to-all | bytes 2359296 | tf_op jit(solution)/shard_map/all_to_all | solution.py:170
  82.5 20.8 %all_to_all.21 = bf16[8,32,2304]{2,1,0:T(8,128)(2,1)S(1)} all-to-all(bf16[8,32,2304]{2,1,0:T(8,128)(2,1)S(1)} %shard_map.78), channel_id=1, replica_groups={{0,2,4,6,8,10,12,14},{1,3,5,7,9,11,13,15},{16,18,20,22,24,26,28,30},{17..., dimensions={0} | all-to-all | bytes 2359296 | tf_op jit(solution)/shard_map/all_to_all | solution.py:183
  104.1 2.0 %collective-permute-done.10.err_ref.other_ref = bf16[256,2304]{1,0:T(8,128)(2,1)S(1)} collective-permute-done((bf16[256,2304]{1,0:T(8,128)(2,1)S(1)}, bf16[256,2304]{1,0:T(8,128)(2,1)S(1)}, u32[]{:S(2)}, u32[]{:S(2)}) %collective-permute-start.10) | collective-permute-done | bytes 1179680 | tf_op jit(solution)/shard_map/ppermute | solution.py:186
  107.2 1.8 %collective-permute-start.11 = (bf16[2,32,512]{2,1,0:T(8,128)(2,1)S(1)}, bf16[2,32,512]{2,1,0:T(8,128)(2,1)S(1)}, u32[]{:S(2)}, u32[]{:S(2)}) collective-permute-start(bf16[2,32,512]{2,1,0:T(8,128)(2,1)S(1)} %get-tuple-element.33), channel_id=1, source_target_pairs={{16,0},{32,16},{48,32},{64,48},{80,64},{96,80},{112,96},{0,112},{1... | collective-permute-start | bytes 196616 | tf_op jit(solution)/shard_map/ppermute | solution.py:209
  109.1 2.2 %collective-permute-done.14 = bf16[2,32,512]{2,1,0:T(8,128)(2,1)S(1)} collective-permute-done((bf16[2,32,512]{2,1,0:T(8,128)(2,1)S(1)}, bf16[2,32,512]{2,1,0:T(8,128)(2,1)S(1)}, u32[]{:S(2)}, u32[]{:S(2)}) %collective-permute-start.14) | collective-permute-done | bytes 65568 | tf_op jit(solution)/shard_map/ppermute | solution.py:208
  111.6 4.0 %collective-permute-done.15 = bf16[2,32,512]{2,1,0:T(8,128)(2,1)S(1)} collective-permute-done((bf16[2,32,512]{2,1,0:T(8,128)(2,1)S(1)}, bf16[2,32,512]{2,1,0:T(8,128)(2,1)S(1)}, u32[]{:S(2)}, u32[]{:S(2)}) %collective-permute-start.15) | collective-permute-done | bytes 65568 | tf_op jit(solution)/shard_map/ppermute | solution.py:211
  115.7 2.7 %collective-permute-start.12 = (bf16[2,32,512]{2,1,0:T(8,128)(2,1)S(1)}, bf16[2,32,512]{2,1,0:T(8,128)(2,1)S(1)}, u32[]{:S(2)}, u32[]{:S(2)}) collective-permute-start(bf16[2,32,512]{2,1,0:T(8,128)(2,1)S(1)} %get-tuple-element.31), channel_id=1, source_target_pairs={{16,0},{32,16},{48,32},{64,48},{80,64},{96,80},{112,96},{0,112},{1... | collective-permute-start | bytes 196616 | tf_op jit(solution)/shard_map/ppermute | solution.py:212
  118.4 1.9 %collective-permute-done.12 = bf16[2,32,512]{2,1,0:T(8,128)(2,1)S(1)} collective-permute-done((bf16[2,32,512]{2,1,0:T(8,128)(2,1)S(1)}, bf16[2,32,512]{2,1,0:T(8,128)(2,1)S(1)}, u32[]{:S(2)}, u32[]{:S(2)}) %collective-permute-start.12) | collective-permute-done | bytes 65568 | tf_op jit(solution)/shard_map/ppermute | solution.py:212
  120.3 2.4 %collective-permute-done.16 = bf16[2,32,512]{2,1,0:T(8,128)(2,1)S(1)} collective-permute-done((bf16[2,32,512]{2,1,0:T(8,128)(2,1)S(1)}, bf16[2,32,512]{2,1,0:T(8,128)(2,1)S(1)}, u32[]{:S(2)}, u32[]{:S(2)}) %collective-permute-start.16) | collective-permute-done | bytes 65568 | tf_op jit(solution)/shard_map/ppermute | solution.py:211
  125.4 1.7 %collective-permute-done.13 = bf16[2,32,512]{2,1,0:T(8,128)(2,1)S(1)} collective-permute-done((bf16[2,32,512]{2,1,0:T(8,128)(2,1)S(1)}, bf16[2,32,512]{2,1,0:T(8,128)(2,1)S(1)}, u32[]{:S(2)}, u32[]{:S(2)}) %collective-permute-start.13) | collective-permute-done | bytes 65568 | tf_op jit(solution)/shard_map/ppermute | solution.py:212
  128.3 3.1 %shard_map.81 = bf16[512,2304]{1,0:T(8,128)(2,1)} custom-call(s32[1]{0:T(128)} %bitcast.core_ref, bf16[512,512]{1,0:T(8,128)(2,1)S(1)} %bitcast.114, bf16[256,2304]{1,0:T(8,128)(2,1)S(1)} %bitcast.110, bf16[256,2304]{1,0:T(8,128)(2,1)S(1)} %collective-permute-done.10.err_ref.other_ref), custom_call_target="tpu_custom_call" | custom-call | flops 1207959552 | bytes 10616832 | tf_op jit(solution)/shard_map/pallas_call | solution.py:49
  132.1 17.2 %all_to_all.22 = bf16[16,32,512]{2,1,0:T(8,128)(2,1)S(1)} all-to-all(bf16[16,32,512]{2,1,0:T(8,128)(2,1)S(1)} %broadcast_in_dim.7), channel_id=1, replica_groups=mesh['layer'=16,'latent'=16] {'layer'}, dimensions={0} | all-to-all | bytes 1048576 | tf_op jit(solution)/shard_map/all_to_all | solution.py:25
  149.3 2.6 %shard_map.82 = bf16[2304,512]{1,0:T(8,128)(2,1)} custom-call(bf16[2304,512]{1,0:T(8,128)(2,1)S(1)} %bitcast.111, bf16[512,512]{1,0:T(8,128)(2,1)S(1)} %bitcast.121), custom_call_target="tpu_custom_call" | custom-call | flops 1207959552 | bytes 10616832 | tf_op jit(solution)/shard_map/pallas_call | solution.py:49
  (69 shorter events, 26.4 us)
Async XLA Ops:
  2.9 5.4 %collective-permute-start.3 = (f32[64,512]{1,0:T(8,128)S(1)}, f32[64,512]{1,0:T(8,128)S(1)}, u32[]{:S(2)}, u32[]{:S(2)}) collective-permute-start(f32[64,512]{1,0:T(8,128)S(1)} %fusion.14), channel_id=1, source_target_pairs={{0,16},{16,32},{32,48},{48,64},{64,80},{80,96},{96,112},{112,0},{1... | collective-permute-start | bytes 393224 | tf_op jit(solution)/shard_map/ppermute | solution.py:142
  7.1 5.2 %collective-permute-start = (f32[64,512]{1,0:T(8,128)S(1)}, f32[64,512]{1,0:T(8,128)S(1)}, u32[]{:S(2)}, u32[]{:S(2)}) collective-permute-start(f32[64,512]{1,0:T(8,128)S(1)} %fusion.12), channel_id=1, source_target_pairs={{16,0},{32,16},{48,32},{64,48},{80,64},{96,80},{112,96},{0,112},{1... | collective-permute-start | bytes 393224 | tf_op jit(solution)/shard_map/ppermute | solution.py:142
  8.8 7.4 %collective-permute-start.4 = (f32[64,512]{1,0:T(8,128)S(1)}, f32[64,512]{1,0:T(8,128)S(1)}, u32[]{:S(2)}, u32[]{:S(2)}) collective-permute-start(f32[64,512]{1,0:T(8,128)S(1)} %fusion.19), channel_id=1, source_target_pairs={{0,16},{16,32},{32,48},{48,64},{64,80},{80,96},{96,112},{112,0},{1... | collective-permute-start | bytes 393224 | tf_op jit(solution)/shard_map/ppermute | solution.py:144
  12.8 6.2 %collective-permute-start.1 = (f32[64,512]{1,0:T(8,128)S(1)}, f32[64,512]{1,0:T(8,128)S(1)}, u32[]{:S(2)}, u32[]{:S(2)}) collective-permute-start(f32[64,512]{1,0:T(8,128)S(1)} %fusion.16), channel_id=1, source_target_pairs={{16,0},{32,16},{48,32},{64,48},{80,64},{96,80},{112,96},{0,112},{1... | collective-permute-start | bytes 393224 | tf_op jit(solution)/shard_map/ppermute | solution.py:144
  16.3 6.0 %collective-permute-start.5 = (f32[64,512]{1,0:T(8,128)S(1)}, f32[64,512]{1,0:T(8,128)S(1)}, u32[]{:S(2)}, u32[]{:S(2)}) collective-permute-start(f32[64,512]{1,0:T(8,128)S(1)} %add.213), channel_id=1, source_target_pairs={{0,16},{16,32},{32,48},{48,64},{64,80},{80,96},{96,112},{112,0},{1... | collective-permute-start | bytes 393224 | tf_op jit(solution)/shard_map/ppermute | solution.py:146
  19.0 7.0 %collective-permute-start.2 = (f32[64,512]{1,0:T(8,128)S(1)}, f32[64,512]{1,0:T(8,128)S(1)}, u32[]{:S(2)}, u32[]{:S(2)}) collective-permute-start(f32[64,512]{1,0:T(8,128)S(1)} %add.201), channel_id=1, source_target_pairs={{16,0},{32,16},{48,32},{64,48},{80,64},{96,80},{112,96},{0,112},{1... | collective-permute-start | bytes 393224 | tf_op jit(solution)/shard_map/ppermute | solution.py:146
  22.3 5.5 %collective-permute-start.6 = (f32[32,512]{1,0:T(8,128)S(1)}, f32[32,512]{1,0:T(8,128)S(1)}, u32[]{:S(2)}, u32[]{:S(2)}) collective-permute-start(f32[32,512]{1,0:T(8,128)S(1)} %get-tuple-element.35), channel_id=1, source_target_pairs={{0,144},{16,160},{32,176},{48,192},{64,208},{80,224},{96,240},{112... | collective-permute-start | bytes 196616 | tf_op jit(solution)/shard_map/ppermute | solution.py:154
  22.7 5.9 %collective-permute-start.7 = (f32[32,512]{1,0:T(8,128)S(1)}, f32[32,512]{1,0:T(8,128)S(1)}, u32[]{:S(2)}, u32[]{:S(2)}) collective-permute-start(f32[32,512]{1,0:T(8,128)S(1)} %get-tuple-element.34), channel_id=1, source_target_pairs={{0,16},{16,32},{32,48},{48,64},{64,80},{80,96},{96,112},{112,0},{1... | collective-permute-start | bytes 196616 | tf_op jit(solution)/shard_map/ppermute | solution.py:155
  26.0 4.4 %collective-permute-start.8 = (f32[32,512]{1,0:T(8,128)S(1)}, f32[32,512]{1,0:T(8,128)S(1)}, u32[]{:S(2)}, u32[]{:S(2)}) collective-permute-start(f32[32,512]{1,0:T(8,128)S(1)} %dynamic-slice_bitcast_fusion.3), channel_id=1, source_target_pairs={{0,128},{16,144},{32,160},{48,176},{64,192},{80,208},{96,224},{112... | collective-permute-start | bytes 196616 | tf_op jit(solution)/shard_map/ppermute | solution.py:156
  31.3 20.1 %all-to-all-start = ((bf16[16,32,512]{2,1,0:T(8,128)(2,1)}), bf16[16,32,512]{2,1,0:T(8,128)(2,1)S(1)}, u32[]{:S(2)}, u32[]{:S(2)}) async-start(bf16[16,32,512]{2,1,0:T(8,128)(2,1)} %broadcast_in_dim.5), calls=%async_computation | async-start | bytes 1048576 | tf_op jit(solution)/shard_map/all_to_all | solution.py:25
  53.8 2.9 %collective-permute-start.9 = (bf16[256,2304]{1,0:T(8,128)(2,1)S(1)}, bf16[256,2304]{1,0:T(8,128)(2,1)S(1)}, u32[]{:S(2)}, u32[]{:S(2)}) collective-permute-start(bf16[256,2304]{1,0:T(8,128)(2,1)S(1)} %shard_map.76), channel_id=1, source_target_pairs={{0,1},{1,0},{2,3},{3,2},{4,5},{5,4},{6,7},{7,6},{8,9},{9,8},{10,11... | collective-permute-start | bytes 3538952 | tf_op jit(solution)/shard_map/ppermute | solution.py:168
  57.5 24.8 %copy-start.4 = (f32[1,2304]{1,0:T(1,128)S(1)}, f32[1,2304]{1,0:T(1,128)}, u32[]{:S(2)}) copy-start(f32[1,2304]{1,0:T(1,128)} %bias_ref.1) | copy-start | bytes 27652
  82.3 21.0 %copy-start.2 = (bf16[512,1,2304]{2,0,1:T(8,128)(2,1)S(1)}, bf16[512,1,2304]{2,0,1:T(8,128)(2,1)}, u32[]{:S(2)}) copy-start(bf16[512,1,2304]{2,0,1:T(8,128)(2,1)} %param.7) | copy-start | bytes 7077892
  103.3 2.8 %collective-permute-start.10 = (bf16[256,2304]{1,0:T(8,128)(2,1)S(1)}, bf16[256,2304]{1,0:T(8,128)(2,1)S(1)}, u32[]{:S(2)}, u32[]{:S(2)}) collective-permute-start(bf16[256,2304]{1,0:T(8,128)(2,1)S(1)} %bitcast.108), channel_id=1, source_target_pairs={{0,1},{1,0},{2,3},{3,2},{4,5},{5,4},{6,7},{7,6},{8,9},{9,8},{10,11... | collective-permute-start | bytes 3538952 | tf_op jit(solution)/shard_map/ppermute | solution.py:186
  107.0 4.3 %collective-permute-start.14 = (bf16[2,32,512]{2,1,0:T(8,128)(2,1)S(1)}, bf16[2,32,512]{2,1,0:T(8,128)(2,1)S(1)}, u32[]{:S(2)}, u32[]{:S(2)}) collective-permute-start(bf16[2,32,512]{2,1,0:T(8,128)(2,1)S(1)} %get-tuple-element.32), channel_id=1, source_target_pairs={{0,16},{16,32},{32,48},{48,64},{64,80},{80,96},{96,112},{112,0},{1... | collective-permute-start | bytes 196616 | tf_op jit(solution)/shard_map/ppermute | solution.py:208
  107.2 4.4 %collective-permute-start.11 = (bf16[2,32,512]{2,1,0:T(8,128)(2,1)S(1)}, bf16[2,32,512]{2,1,0:T(8,128)(2,1)S(1)}, u32[]{:S(2)}, u32[]{:S(2)}) collective-permute-start(bf16[2,32,512]{2,1,0:T(8,128)(2,1)S(1)} %get-tuple-element.33), channel_id=1, source_target_pairs={{16,0},{32,16},{48,32},{64,48},{80,64},{96,80},{112,96},{0,112},{1... | collective-permute-start | bytes 196616 | tf_op jit(solution)/shard_map/ppermute | solution.py:209
  111.3 4.3 %collective-permute-start.15 = (bf16[2,32,512]{2,1,0:T(8,128)(2,1)S(1)}, bf16[2,32,512]{2,1,0:T(8,128)(2,1)S(1)}, u32[]{:S(2)}, u32[]{:S(2)}) collective-permute-start(bf16[2,32,512]{2,1,0:T(8,128)(2,1)S(1)} %fusion.24), channel_id=1, source_target_pairs={{0,16},{16,32},{32,48},{48,64},{64,80},{80,96},{96,112},{112,0},{1... | collective-permute-start | bytes 196616 | tf_op jit(solution)/shard_map/ppermute | solution.py:211
  115.7 4.6 %collective-permute-start.12 = (bf16[2,32,512]{2,1,0:T(8,128)(2,1)S(1)}, bf16[2,32,512]{2,1,0:T(8,128)(2,1)S(1)}, u32[]{:S(2)}, u32[]{:S(2)}) collective-permute-start(bf16[2,32,512]{2,1,0:T(8,128)(2,1)S(1)} %get-tuple-element.31), channel_id=1, source_target_pairs={{16,0},{32,16},{48,32},{64,48},{80,64},{96,80},{112,96},{0,112},{1... | collective-permute-start | bytes 196616 | tf_op jit(solution)/shard_map/ppermute | solution.py:212
  118.4 4.3 %collective-permute-start.16 = (bf16[2,32,512]{2,1,0:T(8,128)(2,1)S(1)}, bf16[2,32,512]{2,1,0:T(8,128)(2,1)S(1)}, u32[]{:S(2)}, u32[]{:S(2)}) collective-permute-start(bf16[2,32,512]{2,1,0:T(8,128)(2,1)S(1)} %get-tuple-element.30), channel_id=1, source_target_pairs={{0,16},{16,32},{32,48},{48,64},{64,80},{80,96},{96,112},{112,0},{1... | collective-permute-start | bytes 196616 | tf_op jit(solution)/shard_map/ppermute | solution.py:211
  122.7 4.3 %collective-permute-start.13 = (bf16[2,32,512]{2,1,0:T(8,128)(2,1)S(1)}, bf16[2,32,512]{2,1,0:T(8,128)(2,1)S(1)}, u32[]{:S(2)}, u32[]{:S(2)}) collective-permute-start(bf16[2,32,512]{2,1,0:T(8,128)(2,1)S(1)} %get-tuple-element.29), channel_id=1, source_target_pairs={{16,0},{32,16},{48,32},{64,48},{80,64},{96,80},{112,96},{0,112},{1... | collective-permute-start | bytes 196616 | tf_op jit(solution)/shard_map/ppermute | solution.py:212
  124.1 7.3 %collective-permute-start.17 = (bf16[32,512]{1,0:T(8,128)(2,1)S(1)}, bf16[32,512]{1,0:T(8,128)(2,1)S(1)}, u32[]{:S(2)}, u32[]{:S(2)}) collective-permute-start(bf16[32,512]{1,0:T(8,128)(2,1)S(1)} %get-tuple-element.36), channel_id=1, source_target_pairs={{0,144},{16,160},{32,176},{48,192},{64,208},{80,224},{96,240},{112... | collective-permute-start | bytes 98312 | tf_op jit(solution)/shard_map/ppermute | solution.py:216
  125.4 6.0 %collective-permute-start.18 = (bf16[32,512]{1,0:T(8,128)(2,1)S(1)}, bf16[32,512]{1,0:T(8,128)(2,1)S(1)}, u32[]{:S(2)}, u32[]{:S(2)}) collective-permute-start(bf16[32,512]{1,0:T(8,128)(2,1)S(1)} %get-tuple-element.37), channel_id=1, source_target_pairs={{0,16},{16,32},{32,48},{48,64},{64,80},{80,96},{96,112},{112,0},{1... | collective-permute-start | bytes 98312 | tf_op jit(solution)/shard_map/ppermute | solution.py:217
  127.1 22.2 %copy-start.3 = (bf16[512,1,2304]{0,2,1:T(8,128)(2,1)S(1)}, bf16[512,1,2304]{0,2,1:T(8,128)(2,1)}, u32[]{:S(2)}) copy-start(bf16[512,1,2304]{0,2,1:T(8,128)(2,1)} %copy.8) | copy-start | bytes 7077892
  127.1 4.3 %collective-permute-start.19 = (bf16[32,512]{1,0:T(8,128)(2,1)S(1)}, bf16[32,512]{1,0:T(8,128)(2,1)S(1)}, u32[]{:S(2)}, u32[]{:S(2)}) collective-permute-start(bf16[32,512]{1,0:T(8,128)(2,1)S(1)} %fusion.28), channel_id=1, source_target_pairs={{0,128},{16,144},{32,160},{48,176},{64,192},{80,208},{96,224},{112... | collective-permute-start | bytes 98312 | tf_op jit(solution)/shard_map/ppermute | solution.py:218
  (3 other events, 18.6 us)
